TPU v7x, 128 devices: a whole 4x4x4 slice. The times are simulated.
128 devices in a mesh: grp: 2 (over x_lo), row: 8 (over y, core), col: 8 (over x_hi, z).
Axes of the slice: x: 4 (x_hi: 2, x_lo: 2; x = x_hi * 2 + x_lo), y: 4, z: 4, core: 2. Of those that a mesh axis runs over, the one named last changes fastest.
Arguments:
- teacher_image: bfloat16 [16384, 1024], P(('grp', 'row', 'col')), may hold values from -4 to 4
- student_image: bfloat16 [16384, 512], P(('grp', 'row', 'col')), may hold values from -4 to 4
- teacher_text: bfloat16 [16384, 1024], P(('grp', 'row', 'col')), may hold values from -4 to 4
- student_text: bfloat16 [16384, 512], P(('grp', 'row', 'col')), may hold values from -4 to 4
Outputs:
- grad_student_image: float32 [16384, 512], P(('grp', 'row', 'col'))
- grad_student_text: float32 [16384, 512], P(('grp', 'row', 'col'))
All inputs are finite; a program needn't handle non-finite values.
Results may differ from a plain program's by a relative error of at most 0.0071.
Values may be sent and summed in bfloat16 or wider, within the bound.
A program may use at most 64 MiB of HBM per device.

v0:
```python
import jax
import jax.numpy as jnp
from jax import lax
from jax.sharding import PartitionSpec as P

EPS = 1e-06
LOGIT_SCALE = 14.285714285714286


def unit_rows(raw):
    values = raw.astype(jnp.float32)
    inverse = lax.rsqrt(jnp.sum(values * values, axis=1, keepdims=True) + EPS)
    return (values * inverse, inverse)


def logits(left, right):
    return LOGIT_SCALE * jnp.dot(left, right.T, preferred_element_type=jnp.float32)


def per_device(teacher_image, student_image, teacher_text, student_text):
    image_teach, image_stud = (
        lax.all_gather(teacher_image, ("grp", "col"), axis=0, tiled=True),
        lax.all_gather(student_image, ("grp", "col"), axis=0, tiled=True),
    )
    text_teach, text_stud = (
        lax.all_gather(teacher_text, "row", axis=0, tiled=True),
        lax.all_gather(student_text, "row", axis=0, tiled=True),
    )
    norm_si, inv_si = unit_rows(image_stud)
    norm_st, inv_st = unit_rows(text_stud)
    norm_ti, inv_ti = unit_rows(image_teach)
    norm_tt, inv_tt = unit_rows(text_teach)
    unit_si = norm_si.astype(jnp.bfloat16)
    unit_st = norm_st.astype(jnp.bfloat16)
    unit_ti = norm_ti.astype(jnp.bfloat16)
    unit_tt = norm_tt.astype(jnp.bfloat16)
    tile_rows = unit_si.shape[0]
    tile_cols = unit_st.shape[0]
    own_count = student_image.shape[0]
    block = min(512, tile_rows)
    count = tile_rows // block
    stud_blocks = unit_si.reshape(count, block, unit_si.shape[1])
    teach_blocks = unit_ti.reshape(count, block, unit_ti.shape[1])

    def first_pass(carry, pieces):
        exp_student = jnp.exp(logits(pieces[0], unit_st))
        exp_teacher = jnp.exp(logits(pieces[1], unit_tt))
        new_carry = (
            carry[0] + jnp.sum(exp_student, axis=0),
            carry[1] + jnp.sum(exp_teacher, axis=0),
        )
        return (new_carry, (jnp.sum(exp_student, axis=1), jnp.sum(exp_teacher, axis=1)))

    zero_cols = jnp.zeros((tile_cols,), jnp.float32)
    col_parts, row_parts = lax.scan(first_pass, (zero_cols, zero_cols), (stud_blocks, teach_blocks))
    row_student = row_parts[0].reshape(tile_rows)
    row_teacher = row_parts[1].reshape(tile_rows)
    col_student, col_teacher = col_parts
    col_place = lax.axis_index("grp") * lax.axis_size("col") + lax.axis_index("col")
    text_place = lax.axis_index("row")
    row_student, row_teacher = lax.psum((row_student, row_teacher), ("grp", "col"))
    col_student, col_teacher = lax.psum((col_student, col_teacher), "row")
    inv_cs = 1.0 / col_student
    inv_ct = 1.0 / col_teacher
    inv_rs = (1.0 / row_student).reshape(count, block)
    inv_rt = (1.0 / row_teacher).reshape(count, block)

    def second_pass(carry, pieces):
        stud_piece, teach_piece, rs_piece, rt_piece = pieces
        exp_student = jnp.exp(logits(stud_piece, unit_st))
        exp_teacher = jnp.exp(logits(teach_piece, unit_tt))
        weight = (
            0.5
            * LOGIT_SCALE
            * (
                exp_student * (rs_piece[:, None] + inv_cs[None, :])
                - exp_teacher * (rt_piece[:, None] + inv_ct[None, :])
            )
        )
        weight = weight.astype(jnp.bfloat16)
        image_piece = jnp.dot(weight, unit_st, preferred_element_type=jnp.float32)
        return (
            carry + jnp.dot(weight.T, stud_piece, preferred_element_type=jnp.float32),
            image_piece,
        )

    zero_text = jnp.zeros((tile_cols, unit_st.shape[1]), jnp.float32)
    text_terms, image_terms = lax.scan(
        second_pass, zero_text, (stud_blocks, teach_blocks, inv_rs, inv_rt)
    )
    image_terms = image_terms.reshape(tile_rows, unit_si.shape[1])
    image_start = col_place * own_count
    text_start = text_place * own_count
    own_image = lax.dynamic_slice_in_dim(norm_si, image_start, own_count, 0)
    own_text = lax.dynamic_slice_in_dim(norm_st, text_start, own_count, 0)
    own_inv_image = lax.dynamic_slice_in_dim(inv_si, image_start, own_count, 0)
    own_inv_text = lax.dynamic_slice_in_dim(inv_st, text_start, own_count, 0)
    full_image = lax.psum(image_terms, ("grp", "col"))
    full_text = lax.psum(text_terms, "row")
    share_image = lax.dynamic_slice_in_dim(full_image, image_start, own_count, 0)
    share_text = lax.dynamic_slice_in_dim(full_text, text_start, own_count, 0)
    grad_image = own_inv_image * (
        share_image - own_image * jnp.sum(own_image * share_image, axis=1, keepdims=True)
    )
    grad_text = own_inv_text * (
        share_text - own_text * jnp.sum(own_text * share_text, axis=1, keepdims=True)
    )
    return (grad_image, grad_text)


def solution(mesh):
    return jax.shard_map(
        per_device,
        mesh=mesh,
        in_specs=(
            P(("grp", "row", "col"), None),
            P(("grp", "row", "col"), None),
            P(("grp", "row", "col"), None),
            P(("grp", "row", "col"), None),
        ),
        out_specs=(P(("grp", "row", "col"), None), P(("grp", "row", "col"), None)),
        check_vma=False,
    )
```

profile of v0, /device:TPU:1, one launch (start us, length us, event | category | flops | bytes accessed | tf_op | source)
XLA Modules:
  0.0 552.5 jit_solution(16944864091431731768)
XLA Ops:
  7.9 0.7 all-gather.11.cloned.1.call-update
  10.1 26.7 %all-gather.7.cloned.1.call-done = bf16[1024,512]{1,0:T(8,128)(2,1)} async-done(((bf16[128,512]{1,0:T(8,128)(2,1)}), bf16[1024,512]{1,0:T(8,128)(2,1)}) %all-gather.7.cloned.1.call-update) | async-done | bytes 1048592 | tf_op jit(solution)/shard_map/all_gather | solution.py:27
  36.8 1.5 fusion.28
  38.3 2.9 convert_multiply_fusion.6
  41.2 22.3 %all-gather.11.cloned.1.call-done = bf16[1024,1024]{1,0:T(8,128)(2,1)} async-done(((bf16[128,1024]{1,0:T(8,128)(2,1)}), bf16[1024,1024]{1,0:T(8,128)(2,1)}) %all-gather.11.cloned.1.call-update) | async-done | bytes 2097168 | tf_op jit(solution)/shard_map/all_gather | solution.py:26
  63.5 2.2 fusion.26
  65.8 1.7 fusion.27
  67.5 64.5 %all-gather.5.cloned.1.call-done = bf16[2048,512]{1,0:T(8,128)(2,1)} async-done(((bf16[128,512]{1,0:T(8,128)(2,1)}), bf16[2048,512]{1,0:T(8,128)(2,1)}) %all-gather.5.cloned.1.call-update) | async-done | bytes 2097168 | tf_op jit(solution)/shard_map/all_gather | solution.py:23
  132.0 2.2 fusion.25
  134.2 3.1 fusion.30
  137.4 79.0 %all-gather.9.cloned.1.call-done = bf16[2048,1024]{1,0:T(8,128)(2,1)} async-done(((bf16[128,1024]{1,0:T(8,128)(2,1)}), bf16[2048,1024]{1,0:T(8,128)(2,1)}) %all-gather.9.cloned.1.call-update) | async-done | bytes 4194320 | tf_op jit(solution)/shard_map/all_gather | solution.py:22
  216.4 3.2 fusion.23
  219.8 2.7 fusion.24
  222.6 21.7 %while.30 = (s32[]{:T(128)}, f32[1024]{0:T(1024)S(1)}, f32[1024]{0:T(1024)S(1)}, f32[4,512]{1,0:T(4,128)S(1)}, f32[4,512]{1,0:T(4,128)S(1)}, /*index=5*/bf16[4,5...) while((s32[]{:T(128)}, f32[1024]{0:T(1024)S(1)}, ...), condition=%wide.region_9.10_spmd.clone, body=%wide.region_4.9_spmd.clone.sunk | while | flops 1613759488 | bytes 4763791 | solution.py:55
  222.6 3.4 fusion.54
  226.0 1.9 fusion.55
  228.0 3.4 fusion.54
  231.4 1.9 fusion.55
  233.4 3.4 fusion.54
  236.8 1.9 fusion.55
  238.8 3.4 fusion.54
  242.2 1.9 fusion.55
  244.3 60.0 %all-reduce = (f32[2048]{0:T(1024)S(1)}, f32[2048]{0:T(1024)S(1)}) all-reduce(f32[2048]{0:T(1024)S(1)} %bitcast.82, f32[2048]{0:T(1024)S(1)} %bitcast.81), channel_id=1, replica_groups=mesh['grp'=2,'row'=8,'col'=8] {'grp','col'}, use_global_device_ids=true, to_apply=%region_10.11 | all-reduce | flops 4096 | bytes 32768 | tf_op jit(solution)/shard_map/psum | solution.py:61
  304.3 36.6 %all-reduce.1 = (f32[1024]{0:T(1024)S(1)}, f32[1024]{0:T(1024)S(1)}) all-reduce(f32[1024]{0:T(1024)S(1)} %get-tuple-element.111, f32[1024]{0:T(1024)S(1)} %get-tuple-element.113), channel_id=1, replica_groups=mesh['grp'=2,'row'=8,'col'=8] {'row'}, use_global_device_ids=true, to_apply=%region_12.13 | all-reduce | flops 2048 | bytes 16384 | tf_op jit(solution)/shard_map/psum | solution.py:62
  340.9 28.9 %while.31 = (s32[]{:T(128)}, f32[1024,512]{1,0:T(8,128)S(1)}, f32[4,512,512]{2,1,0:T(8,128)}, bf16[4,512,512]{2,1,0:T(8,128)(2,1)}, bf16[1024,512]{1,0:T(8,128)(...) while((s32[]{:T(128)}, f32[1024,512]{1,0:T(8,128)S(1)}, ...), condition=%wide.region_15.16_spmd.clone, body=%wide.region_14.15_spmd.clone.sunk | while | flops 2690121728 | bytes 27283644 | solution.py:88
  340.9 3.3 fusion.64
  344.3 1.2 multiply_convert_fusion.2
  345.5 0.9 select_add_fusion.6
  346.4 1.7 fusion.65
  348.1 3.3 fusion.64
  351.5 1.2 multiply_convert_fusion.2
  352.7 0.9 select_add_fusion.6
  353.6 1.7 fusion.65
  355.4 3.3 fusion.64
  358.7 1.2 multiply_convert_fusion.2
  360.0 0.9 select_add_fusion.6
  360.9 1.7 fusion.65
  362.6 3.3 fusion.64
  366.0 1.2 multiply_convert_fusion.2
  367.2 0.9 select_add_fusion.6
  368.1 1.7 fusion.65
  369.8 1.3 copy-done
  371.9 62.6 %all-reduce.7.cloned.1.call-done = f32[1024,512]{1,0:T(8,128)} async-done(((f32[1024,512]{1,0:T(8,128)}), f32[1024,512]{1,0:T(8,128)}) %all-reduce.7.cloned.1.call-update) | async-done | bytes 2097168 | tf_op jit(solution)/shard_map/psum | solution.py:99
  434.5 1.1 multiply_reduce_fusion
  435.7 1.8 subtract_multiply_fusion
  437.5 105.1 %all-reduce.5.cloned.1.call-done = f32[2048,512]{1,0:T(8,128)} async-done(((f32[2048,512]{1,0:T(8,128)}), f32[2048,512]{1,0:T(8,128)}) %all-reduce.5.cloned.1.call-update) | async-done | bytes 4194320 | tf_op jit(solution)/shard_map/psum | solution.py:98
  542.6 1.1 multiply_reduce_fusion.1
  543.8 1.8 subtract_multiply_fusion.1
  (60 shorter events, 3.6 us)
Async XLA Ops:
  7.2 29.6 %all-gather.7.cloned.1.call-start = ((), (), s32[]{:S(2)}) async-start(), calls=%async_computation.1 | async-start | bytes 1179648 | tf_op jit(solution)/shard_map/all_gather | solution.py:27
  7.9 55.6 %all-gather.11.cloned.1.call-start = ((), (), s32[]{:S(2)}) async-start(), calls=%async_computation.3 | async-start | bytes 2359296 | tf_op jit(solution)/shard_map/all_gather | solution.py:26
  8.6 123.3 %all-gather.5.cloned.1.call-start = ((), (), s32[]{:S(2)}) async-start(), calls=%async_computation | async-start | bytes 2228224 | tf_op jit(solution)/shard_map/all_gather | solution.py:23
  9.4 207.0 %all-gather.9.cloned.1.call-start = ((), (), s32[]{:S(2)}) async-start(), calls=%async_computation.2 | async-start | bytes 4456448 | tf_op jit(solution)/shard_map/all_gather | solution.py:22
  10.0 424.6 %all-reduce.7.cloned.1.call-start = ((), (), s32[]{:S(2)}) async-start(), calls=%async_computation.5 | async-start | bytes 4194304 | tf_op jit(solution)/shard_map/psum | solution.py:99
  63.5 2.2 copy-start.4
  132.0 2.2 copy-start.3
  216.4 3.4 copy-start.1
  340.9 3.4 copy-start.2
  348.1 3.4 copy-start.2
  355.4 3.4 copy-start.2
  362.6 3.4 copy-start.2
  369.8 1.4 copy-start
  371.2 171.4 %all-reduce.5.cloned.1.call-start = ((), (), s32[]{:S(2)}) async-start(), calls=%async_computation.4 | async-start | bytes 8388608 | tf_op jit(solution)/shard_map/psum | solution.py:98
Sparse Core Ops, SparseCore 0:
  9.7 26.9 all-gather.6
  38.5 25.0 all-gather.10
  65.2 66.7 all-gather.4
  133.5 82.8 all-gather.8
  371.3 63.1 all-reduce.6
  437.8 104.8 all-reduce.4
where the time goes:
time: 553 us; the launch traced here: 552 us
  waiting for transfers between devices  363 us (66%)
  blocking collectives  96.6 us (17%)
  matrix products  49.9 us (9%)
  other arithmetic  25.7 us (5%)
  between operations  14.3 us (3%)
    psum x1, waiting for transfers between devices, per_device(): full_image = lax.psum(image_terms, ('grp', 'col'))  105 us
    all_gather x1, waiting for transfers between devices, per_device(): lax.all_gather(teacher_image, ('grp', 'col'), axis=0, tiled=True)  79 us
    all_gather x1, waiting for transfers between devices, per_device(): lax.all_gather(student_image, ('grp', 'col'), axis=0, tiled=True)  64.5 us
    psum x1, waiting for transfers between devices, per_device(): full_text = lax.psum(text_terms, 'row')  62.6 us
    psum x1, blocking collectives, per_device(): lax.psum((row_student, row_teacher), ('grp', 'col'))  60 us
    dot_general x16, matrix products, logits(): jnp.dot(left, right.T, preferred_element_type=jnp.float32)  39.4 us
    psum x1, blocking collectives, per_device(): col_student, col_teacher = lax.psum((col_student, col_teacher), 'row')  36.6 us
    all_gather x1, waiting for transfers between devices, per_device(): lax.all_gather(student_text, 'row', axis=0, tiled=True)  26.7 us
  transfers between devices with their start and end apart: 6, of which 6 were waited for; matrix products, arithmetic and copies ran while one was open for 3% of the time, Pallas kernels for 0%

commit v1 on v0

v1 whole, which is shorter than its diff:
```python
import jax
import jax.numpy as jnp
from jax import lax
from jax.experimental import pallas as pl
from jax.experimental.pallas import tpu as pltpu
from jax.sharding import PartitionSpec as P

EPS = 1e-06
LOGIT_SCALE = 14.285714285714286
LOG2E = 1.4426950408889634
MESH = pl.DeviceIdType.MESH
B = 128

SLOTS = [(0, 0), (0, 1), (1, 0), (3, 0), (2, 0), (1, 1), (3, 1), (2, 1)]
N = len(SLOTS)


def slot_of(step, side):
    return SLOTS.index((step % 4, side % 2))


def minus(a, b):
    return slot_of(SLOTS[a][0] - SLOTS[b][0], SLOTS[a][1] - SLOTS[b][1])


PLUS, MINUS, PAIR = (1, 0), (3, 0), (0, 1)
OWN = [(0, 1, PAIR), (0, 3, PLUS), (0, 2, MINUS)]
HOPS = [(s, d, to, piece) for piece in ("T0", "T1", "S") for s, d, to in OWN]
HOPS += [
    (3, 6, PAIR, "T0"),
    (3, 4, PLUS, "T0"),
    (2, 5, PAIR, "T1"),
    (2, 4, MINUS, "T1"),
    (3, 6, PAIR, "T1"),
    (2, 5, PAIR, "T0"),
    (3, 4, PLUS, "S0"),
    (2, 4, MINUS, "S1"),
    (1, 6, PLUS, "S"),
    (1, 5, MINUS, "S"),
    (6, 7, PLUS, "T0"),
    (5, 7, MINUS, "T1"),
    (6, 7, PLUS, "S0"),
    (5, 7, MINUS, "S1"),
]
PIECE_ROWS = {"T0": (0, 64), "T1": (64, 64), "S": (0, 128), "S0": (0, 64), "S1": (64, 64)}
N_HOPS = len(HOPS)


def dot_nt(a, b):
    return lax.dot_general(a, b, (((1,), (1,)), ((), ())), preferred_element_type=jnp.float32)


def unit_rows(raw):
    values = raw.astype(jnp.float32)
    inverse = lax.rsqrt(jnp.sum(values * values, axis=1, keepdims=True) + EPS)
    return values * inverse, inverse


def kernel(
    ti_ref, si_ref, tt_ref, st_ref, gi_ref, gt_ref,
    it, is_, xt, xs, es, et, w, ist,
    row_acc, col_acc, row_inv, col_inv,
    isum, isum_in, tsum, tsum_sib, csum, tsum_in,
    di, di_in, own_di, dt_keep, dt_other, dt_sib, dt_out, dt_in,
    hop_send, hop_recv, sib_send, sib_recv, sum_send, sum_recv, grad_send, grad_recv, grad_sib_send, grad_sib_recv,
):
    grp, row, col = lax.axis_index("grp"), lax.axis_index("row"), lax.axis_index("col")
    x_hi, z = col // 4, lax.rem(col, 4)
    y, core = row // 2, lax.rem(row, 2)

    def image_peer(step, side):
        to_grp = 1 - grp if side else grp
        return (to_grp, lax.rem(y + step, 4) * 2 + core, col)

    def text_peer(step, side):
        to_grp = 1 - grp if side else grp
        to_hi = 1 - x_hi if side else x_hi
        return (to_grp, row, to_hi * 4 + lax.rem(z + step, 4))

    peers = (image_peer, text_peer)
    sibling = (grp, y * 2 + 1 - core, col)

    barrier = pltpu.get_barrier_semaphore()
    for peer in peers:
        for slot in range(1, N):
            pl.semaphore_signal(barrier, inc=1, device_id=peer(*SLOTS[slot]), device_id_type=MESH)
    pl.semaphore_signal(barrier, inc=1, device_id=sibling, device_id_type=MESH)

    it[0:B, :] = unit_rows(ti_ref[...])[0].astype(jnp.bfloat16)
    xt[0:B, :] = unit_rows(tt_ref[...])[0].astype(jnp.bfloat16)
    is_[0:B, :] = unit_rows(si_ref[...])[0].astype(jnp.bfloat16)
    xs[0:B, :] = unit_rows(st_ref[...])[0].astype(jnp.bfloat16)

    arrays = ((it, is_, 1), (xt, xs, 2))

    def piece_ref(side, slot, piece):
        teach, stud, stride = arrays[side]
        first, rows = PIECE_ROWS[piece]
        ref = teach if piece[0] == "T" else stud
        return ref.at[pl.ds(slot * stride * B + first, rows), :]

    def hop(side, i):
        src, dst, to, piece = HOPS[i]
        return pltpu.make_async_remote_copy(
            src_ref=piece_ref(side, src, piece),
            dst_ref=piece_ref(side, dst, piece),
            send_sem=hop_send.at[side, i],
            recv_sem=hop_recv.at[side, i],
            device_id=peers[side](*to),
            device_id_type=MESH,
        )

    def start(dst, piece):
        for side in (0, 1):
            for i, h in enumerate(HOPS):
                if h[1] == dst and h[3] == piece:
                    hop(side, i).start()

    def arrived(dst, piece, sides=(0, 1)):
        for side in sides:
            for i, h in enumerate(HOPS):
                if h[1] == dst and h[3] == piece:
                    hop(side, i).wait_recv()

    def to_sibling(slot, kind):
        ref = xt if kind == "T" else xs
        k = 0 if kind == "T" else 1
        return pltpu.make_async_remote_copy(
            src_ref=ref.at[pl.ds(2 * slot * B, B), :],
            dst_ref=ref.at[pl.ds((2 * slot + 1) * B, B), :],
            send_sem=sib_send.at[k, slot],
            recv_sem=sib_recv.at[k, slot],
            device_id=sibling,
            device_id_type=MESH,
        )

    pl.semaphore_wait(barrier, 2 * (N - 1) + 1)

    for piece in ("T0", "T1", "S"):
        for dst in (1, 3, 2):
            start(dst, piece)
    to_sibling(0, "T").start()
    to_sibling(0, "S").start()

    row_acc[...] = jnp.zeros_like(row_acc)
    col_acc[...] = jnp.zeros_like(col_acc)

    def logits_tile(mat, r, c):
        left, right, out = ((is_, xs, es), (it, xt, et))[mat]
        r = pl.multiple_of(r, 512)
        c = pl.multiple_of(c, 256)
        x = dot_nt(left[pl.ds(r, 512), :], right[pl.ds(c, 256), :])
        e = jnp.exp2(x * (LOGIT_SCALE * LOG2E))
        out[pl.ds(r, 512), pl.ds(c, 256)] = e
        row_acc[mat, pl.ds(r, 512), :] += e[:, 0:128] + e[:, 128:256]
        col_acc[mat, :, pl.ds(c, 256)] += jnp.sum(e.reshape(64, 8, 256), axis=0)

    def logits(mat, rows, cols):
        n_c = (cols[1] - cols[0]) // 256
        n_r = (rows[1] - rows[0]) // 512

        def body(i, carry):
            logits_tile(mat, rows[0] + lax.rem(i, n_r) * 512, cols[0] + i // n_r * 256)
            return carry

        lax.fori_loop(0, n_c * n_r, body, 0)

    for slot in (1, 3, 2):
        arrived(slot, "T0")
    start(6, "T0")
    for i, h in enumerate(HOPS):
        if h[1] == 4 and h[3] == "T0":
            hop(0, i).start()
            hop(1, i).start()
    for slot in (2, 1, 3):
        arrived(slot, "T1")
    start(5, "T1")
    start(4, "T1")
    start(6, "T1")
    start(5, "T0")
    for slot in (1, 2, 3):
        to_sibling(slot, "T").start()
    for slot in (1, 2, 3):
        arrived(slot, "S")
    start(4, "S0")
    start(4, "S1")
    start(6, "S")
    start(5, "S")
    for slot in (1, 2, 3):
        to_sibling(slot, "S").start()
    for slot in (0, 1, 2, 3):
        to_sibling(slot, "T").wait_recv()
    logits(1, (0, 512), (0, 1024))
    for slot in (0, 1, 2, 3):
        to_sibling(slot, "S").wait_recv()
    logits(0, (0, 512), (0, 1024))
    arrived(6, "T0")
    start(7, "T0")
    arrived(5, "T1")
    start(7, "T1")
    arrived(4, "T0")
    arrived(4, "T1")
    to_sibling(4, "T").start()
    arrived(4, "S0")
    arrived(4, "S1")
    to_sibling(4, "S").start()
    arrived(6, "S")
    start(7, "S0")
    arrived(5, "S")
    start(7, "S1")
    to_sibling(5, "S").start()
    to_sibling(6, "S").start()
    to_sibling(4, "T").wait_recv()
    logits(1, (0, 512), (1024, 1280))
    to_sibling(4, "S").wait_recv()
    logits(0, (0, 512), (1024, 1280))

    for s in range(5):
        ist[:, s * B : (s + 1) * B] = is_[s * B : (s + 1) * B, :].T

    arrived(7, "T0")
    arrived(7, "T1")
    to_sibling(7, "T").start()
    arrived(6, "T1")
    to_sibling(6, "T").start()
    arrived(5, "T0")
    to_sibling(5, "T").start()
    arrived(7, "S0")
    arrived(7, "S1")
    to_sibling(7, "S").start()
    logits(1, (512, 1024), (0, 1280))
    logits(0, (512, 1024), (0, 1280))
    for slot in (5, 6, 7):
        to_sibling(slot, "T").wait_recv()
    logits(1, (0, 1024), (1280, 2048))
    for slot in (5, 6, 7):
        to_sibling(slot, "S").wait_recv()
    logits(0, (0, 1024), (1280, 2048))

    for mat in (0, 1):
        for b in range(2 * N):
            tsum[mat * 16 + b : mat * 16 + b + 1, :] = jnp.sum(
                col_acc[mat, :, b * B : (b + 1) * B], axis=0, keepdims=True
            )
    tsum_to_sib = pltpu.make_async_remote_copy(
        src_ref=tsum, dst_ref=tsum_sib, send_sem=sum_send.at[14], recv_sem=sum_recv.at[14],
        device_id=sibling, device_id_type=MESH,
    )
    tsum_to_sib.start()

    def row_total(i, carry):
        mat, s = i // N, lax.rem(i, N)
        part = row_acc[mat, pl.ds(pl.multiple_of(s * B, B), B), :]
        isum[pl.ds(i, 1), :] = jnp.sum(part.T, axis=0, keepdims=True)
        return carry

    for i in range(2 * N):
        row_total(i, 0)

    def sum_copy(side, slot):
        back = minus(0, slot) - 1
        return pltpu.make_async_remote_copy(
            src_ref=(isum, csum)[side],
            dst_ref=(isum_in, tsum_in)[side].at[back],
            send_sem=sum_send.at[side * 7 + slot - 1],
            recv_sem=sum_recv.at[side * 7 + back],
            device_id=peers[side](*SLOTS[slot]),
            device_id_type=MESH,
        )

    def sum_from(side, slot):
        return pltpu.make_async_remote_copy(
            src_ref=(isum, csum)[side],
            dst_ref=(isum_in, tsum_in)[side].at[slot - 1],
            send_sem=sum_send.at[side * 7 + slot - 1],
            recv_sem=sum_recv.at[side * 7 + slot - 1],
            device_id=peers[side](*SLOTS[slot]),
            device_id_type=MESH,
        )

    tsum_to_sib.wait_recv()
    for mat in (0, 1):
        for s in range(N):
            r = mat * 16 + 2 * s
            csum[r : r + 1, :] = tsum[r : r + 1, :] + tsum_sib[r + 1 : r + 2, :]
            csum[r + 1 : r + 2, :] = tsum[r + 1 : r + 2, :] + tsum_sib[r : r + 1, :]
    for slot in range(N - 1, 0, -1):
        sum_copy(1, slot).start()
    for slot in range(N - 1, 0, -1):
        sum_copy(0, slot).start()

    for s in range(5, N):
        ist[:, s * B : (s + 1) * B] = is_[s * B : (s + 1) * B, :].T

    for slot in range(1, N):
        sum_from(0, slot).wait_recv()
    half = 0.5 * LOGIT_SCALE
    for mat in (0, 1):
        for t in range(N):
            total = isum[mat * N + t : mat * N + t + 1, :]
            for e in range(1, N):
                r = mat * N + minus(t, e)
                total = total + isum_in[e - 1, r : r + 1, :]
            row_inv[mat, t * B : (t + 1) * B, :] = jnp.broadcast_to(half / total, (B, B)).T
    for slot in range(1, N):
        sum_from(1, slot).wait_recv()
    for mat in (0, 1):
        for t in range(N):
            for par in (0, 1):
                r = mat * 16 + 2 * t + par
                total = csum[r : r + 1, :]
                for e in range(1, N):
                    q = mat * 16 + 2 * minus(t, e) + par
                    total = total + tsum_in[e - 1, q : q + 1, :]
                c = (2 * t + par) * B
                col_inv[mat, :, c : c + B] = jnp.broadcast_to(half / total, (8, B))

    def weight_tile(i, carry):
        r = pl.multiple_of(i // 8 * 512, 512)
        c = pl.multiple_of(lax.rem(i, 8) * 256, 256)
        for part in range(2):
            cc = c + part * B
            a = es[pl.ds(r, 512), pl.ds(cc, B)] * (row_inv[0, pl.ds(r, 512), :] + col_inv[0, 0:1, pl.ds(cc, B)])
            b = et[pl.ds(r, 512), pl.ds(cc, B)] * (row_inv[1, pl.ds(r, 512), :] + col_inv[1, 0:1, pl.ds(cc, B)])
            w[pl.ds(r, 512), pl.ds(cc, B)] = (a - b).astype(jnp.bfloat16)
        return carry

    lax.fori_loop(0, 16, weight_tile, 0)

    def grad_copy(side, slot):
        back = minus(0, slot) - 1
        src = di.at[pl.ds(slot * B, B), :] if side == 0 else dt_out.at[slot]
        return pltpu.make_async_remote_copy(
            src_ref=src,
            dst_ref=(di_in, dt_in)[side].at[back],
            send_sem=grad_send.at[side, slot - 1],
            recv_sem=grad_recv.at[side, back],
            device_id=peers[side](*SLOTS[slot]),
            device_id_type=MESH,
        )

    def grad_from(side, slot):
        return pltpu.make_async_remote_copy(
            src_ref=di.at[pl.ds(slot * B, B), :] if side == 0 else dt_out.at[slot],
            dst_ref=(di_in, dt_in)[side].at[slot - 1],
            send_sem=grad_send.at[side, slot - 1],
            recv_sem=grad_recv.at[side, slot - 1],
            device_id=peers[side](*SLOTS[slot]),
            device_id_type=MESH,
        )

    def grad_sib(slot):
        return pltpu.make_async_remote_copy(
            src_ref=dt_other.at[slot], dst_ref=dt_sib.at[slot],
            send_sem=grad_sib_send.at[slot], recv_sem=grad_sib_recv.at[slot],
            device_id=sibling, device_id_type=MESH,
        )

    def text_terms(s):
        out = jnp.dot(ist[...], w[:, 2 * s * B : 2 * (s + 1) * B], preferred_element_type=jnp.float32)
        dt_keep[s] = out[:, 0:B]
        dt_other[s] = out[:, B : 2 * B].astype(jnp.bfloat16)
        grad_sib(s).start()

    def text_send(s):
        grad_sib(s).wait_recv()
        dt_out[s] = (dt_keep[s] + dt_sib[s].astype(jnp.float32)).astype(jnp.bfloat16)
        grad_copy(1, s).start()

    def image_terms(s):
        out = jnp.dot(w[s * B : (s + 2) * B, :], xs[...], preferred_element_type=jnp.float32)
        di[s * B : (s + 2) * B, :] = out.astype(jnp.bfloat16)
        if s == 0:
            own_di[...] = out[0:B, :]
        for t in (s + 1, s):
            if t:
                grad_copy(0, t).start()

    text_terms(7)
    text_terms(4)
    image_terms(6)
    text_send(7)
    text_send(4)
    text_terms(6)
    text_terms(5)
    image_terms(4)
    text_send(6)
    text_send(5)
    text_terms(3)
    text_terms(2)
    image_terms(2)
    text_send(3)
    text_send(2)
    text_terms(1)
    text_terms(0)
    image_terms(0)
    text_send(1)
    grad_sib(0).wait_recv()

    def finish(raw, total):
        norm, inverse = unit_rows(raw)
        return inverse * (total - norm * jnp.sum(norm * total, axis=1, keepdims=True))

    total = own_di[...]
    for slot in range(1, N):
        grad_from(0, slot).wait_recv()
        total = total + di_in[slot - 1].astype(jnp.float32)
    gi_ref[...] = finish(si_ref[...], total)
    total = dt_keep[0] + dt_sib[0].astype(jnp.float32)
    for slot in range(1, N):
        grad_from(1, slot).wait_recv()
        total = total + dt_in[slot - 1].astype(jnp.float32)
    gt_ref[...] = finish(st_ref[...], total.T)

    for side in (0, 1):
        for i in range(N_HOPS):
            hop(side, i).wait_send()
        for slot in range(1, N):
            sum_copy(side, slot).wait_send()
            grad_copy(side, slot).wait_send()
    for slot in range(N):
        to_sibling(slot, "T").wait_send()
        to_sibling(slot, "S").wait_send()
        grad_sib(slot).wait_send()
    tsum_to_sib.wait_send()


def per_device(teacher_image, student_image, teacher_text, student_text):
    f32, bf16 = jnp.float32, jnp.bfloat16
    vmem = pl.BlockSpec(memory_space=pltpu.VMEM)
    dma = pltpu.SemaphoreType.DMA
    return pl.pallas_call(
        kernel,
        out_shape=(jax.ShapeDtypeStruct((B, 512), f32), jax.ShapeDtypeStruct((B, 512), f32)),
        in_specs=[vmem] * 4,
        out_specs=(vmem, vmem),
        scratch_shapes=[
            pltpu.VMEM((N * B, 1024), bf16),
            pltpu.VMEM((N * B, 512), bf16),
            pltpu.VMEM((2 * N * B, 1024), bf16),
            pltpu.VMEM((2 * N * B, 512), bf16),
            pltpu.VMEM((N * B, 2 * N * B), f32),
            pltpu.VMEM((N * B, 2 * N * B), f32),
            pltpu.VMEM((N * B, 2 * N * B), bf16),
            pltpu.VMEM((512, N * B), bf16),
            pltpu.VMEM((2, N * B, B), f32),
            pltpu.VMEM((2, 8, 2 * N * B), f32),
            pltpu.VMEM((2, N * B, B), f32),
            pltpu.VMEM((2, 8, 2 * N * B), f32),
            pltpu.VMEM((16, B), f32),
            pltpu.VMEM((7, 16, B), f32),
            pltpu.VMEM((32, B), f32),
            pltpu.VMEM((32, B), f32),
            pltpu.VMEM((32, B), f32),
            pltpu.VMEM((7, 32, B), f32),
            pltpu.VMEM((N * B, 512), bf16),
            pltpu.VMEM((7, B, 512), bf16),
            pltpu.VMEM((B, 512), f32),
            pltpu.VMEM((N, 512, B), f32),
            pltpu.VMEM((N, 512, B), bf16),
            pltpu.VMEM((N, 512, B), bf16),
            pltpu.VMEM((N, 512, B), bf16),
            pltpu.VMEM((7, 512, B), bf16),
            dma((2, N_HOPS)),
            dma((2, N_HOPS)),
            dma((2, N)),
            dma((2, N)),
            dma((15,)),
            dma((15,)),
            dma((2, 7)),
            dma((2, 7)),
            dma((N,)),
            dma((N,)),
        ],
        compiler_params=pltpu.CompilerParams(
            collective_id=0, has_side_effects=True, vmem_limit_bytes=60 << 20
        ),
        cost_estimate=pl.CostEstimate(flops=10_737_418_240, bytes_accessed=1 << 20, transcendentals=1 << 22),
    )(teacher_image, student_image, teacher_text, student_text)


def solution(mesh):
    spec = P(("grp", "row", "col"), None)
    return jax.shard_map(
        per_device, mesh=mesh, in_specs=(spec,) * 4, out_specs=(spec, spec), check_vma=False
    )
```

time: 553 us -> 72.9 us (0.13)
  waiting for transfers between devices: 363 us -> 0 us
  blocking collectives: 96.6 us -> 0 us
  Pallas kernels: 0 us -> 69.7 us
  matrix products: 49.9 us -> 0 us
  other arithmetic: 25.7 us -> 0 us
  between operations: 14.3 us -> 0.65 us
    all_gather x4 -> x0, waiting for transfers between devices: 193 us -> none  [the longest x1 79 us: per_device(): lax.all_gather(teacher_image, ('grp', 'col'), axis=0, tiled=True)]
    psum x2 -> x0, waiting for transfers between devices: 168 us -> none  [the longest x1 105 us: per_device(): full_image = lax.psum(image_terms, ('grp', 'col'))]
    psum x2 -> x0, blocking collectives: 96.6 us -> none  [the longest x1 60 us: per_device(): lax.psum((row_student, row_teacher), ('grp', 'col'))]
    pallas_call x0 -> x1, Pallas kernels: none -> 69.7 us  [per_device(): pl.pallas_call(kernel, out_shape=(jax.ShapeDtypeStruct((B, 512), f32), ja...]
    dot_general x24 -> x0, matrix products: 49.9 us -> none  [the longest x16 39.4 us: logits(): jnp.dot(left, right.T, preferred_element_type=jnp.float32)]
    reduce_sum x6 -> x0, other arithmetic: 11.4 us -> none  [the longest x4 9.16 us: unit_rows(): inverse = lax.rsqrt(jnp.sum(values * values, axis=1, keepdims=True) + EPS)]
    convert_element_type x3 -> x0, other arithmetic: 7.59 us -> none  [the longest x1 3.13 us: per_device(): unit_si = norm_si.astype(jnp.bfloat16)]
    mul x3 -> x0, other arithmetic: 6.6 us -> none  [the longest x1 2.91 us: unit_rows(): return (values * inverse, inverse)]
  transfers between devices with their start and end apart: 6 -> 0, of which waited for: 6 -> 0; matrix products, arithmetic and copies ran while one was open for 3% -> 0% of each run, Pallas kernels for 0% -> 0%
where the time goes in v1:
time: 72.9 us; the launch traced here: 72.8 us
  Pallas kernels  69.7 us (96%)
  local copies, waits for them, and re-layouts  2.42 us (3%)
    pallas_call x1, Pallas kernels, per_device(): pl.pallas_call(kernel, out_shape=(jax.ShapeDtypeStruct((B, 512), f32), ja...  69.7 us
    unnamed x4, local copies, waits for them, and re-layouts  2.42 us

profile of v1, /device:TPU:1, one launch (start us, length us, event | category | flops | bytes accessed | tf_op | source)
XLA Modules:
  0.0 72.8 jit_solution(1553249127292391686)
XLA Ops:
  0.6 69.7 %shard_map.59 = (f32[128,512]{1,0:T(8,128)}, f32[128,512]{1,0:T(8,128)}) custom-call(bf16[128,1024]{1,0:T(8,128)(2,1)} %ti_ref.1, bf16[128,512]{1,0:T(8,128)(2,1)} %si_ref.1, bf16[128,1024]{1,0:T(8,128)(2,1)} %tt_ref.1, bf16[128,512]{1,0:T(8,128)(2,1)} %st_ref.1), custom_call_target="tpu_custom_call" | custom-call | flops 10737418240 | bytes 1048576 | tf_op jit(solution)/shard_map/pallas_call | solution.py:432
  70.3 0.0 copy-start
  70.4 1.7 %copy.8 = f32[128,512]{1,0:T(8,128)} copy(f32[128,512]{1,0:T(8,128)} %get-tuple-element.4) | data formatting | bytes 524288
  72.1 0.0 copy-done
  72.1 0.7 copy.9
Async XLA Ops:
  70.3 1.7 %copy-start = (f32[128,512]{1,0:T(8,128)S(1)}, f32[128,512]{1,0:T(8,128)}, u32[]{:S(2)}) copy-start(f32[128,512]{1,0:T(8,128)} %get-tuple-element.5) | copy-start | bytes 786436

commit v2 on v0

v2 whole, which is shorter than its diff:
```python
import jax
import jax.numpy as jnp
from jax import lax
from jax.experimental import pallas as pl
from jax.experimental.pallas import tpu as pltpu
from jax.sharding import PartitionSpec as P

EPS = 1e-06
LOGIT_SCALE = 14.285714285714286
LOG2E = 1.4426950408889634
MESH = pl.DeviceIdType.MESH
B = 128
F32, BF16 = jnp.float32, jnp.bfloat16

SLOTS = [(0, 0), (0, 1), (1, 0), (3, 0), (2, 0), (1, 1), (3, 1), (2, 1)]
N = len(SLOTS)
ORDER = [2, 3, 4, 0, 1, 6, 5, 7]
POS = [ORDER.index(s) for s in range(N)]


def slot_of(step, side):
    return SLOTS.index((step % 4, side % 2))


def minus(a, b):
    return slot_of(SLOTS[a][0] - SLOTS[b][0], SLOTS[a][1] - SLOTS[b][1])


PLUS, MINUS, PAIR, ACROSS = (1, 0), (3, 0), (0, 1), (2, 0)
HOPS = [
    (0, 1, PAIR, "S"),
    (0, 3, PLUS, "T0"),
    (0, 2, MINUS, "T0"),
    (0, 1, PAIR, "T0"),
    (0, 3, PLUS, "T1"),
    (0, 2, MINUS, "T1"),
    (0, 3, PLUS, "S"),
    (0, 2, MINUS, "S"),
    (3, 6, PAIR, "T0"),
    (3, 4, PLUS, "T0"),
    (2, 5, PAIR, "T1"),
    (2, 4, MINUS, "T1"),
    (0, 1, PAIR, "T1"),
    (3, 6, PAIR, "T1"),
    (2, 5, PAIR, "T0"),
    (1, 6, PLUS, "S"),
    (1, 5, MINUS, "S"),
    (3, 4, PLUS, "S0"),
    (2, 4, MINUS, "S1"),
    (6, 7, PLUS, "T0"),
    (5, 7, MINUS, "T1"),
    (6, 7, PLUS, "S0"),
    (5, 7, MINUS, "S1"),
]
PIECE_ROWS = {"T0": (0, 64), "T1": (64, 64), "S": (0, 128), "S0": (0, 64), "S1": (64, 64)}
N_HOPS = len(HOPS)
GRAD_TO = {7: PAIR, 5: PLUS, 6: MINUS, 2: PLUS, 3: MINUS, 4: ACROSS, 1: PAIR}
SINKS = {4: (7,), 1: (5, 6), 0: (2, 3, 4, 1)}


def dot_nt(a, b):
    return lax.dot_general(a, b, (((1,), (1,)), ((), ())), preferred_element_type=F32)


def unit_rows(raw):
    values = raw.astype(F32)
    inverse = lax.rsqrt(jnp.sum(values * values, axis=1, keepdims=True) + EPS)
    return values * inverse, inverse


def kernel(
    ti_hbm, si_hbm, tt_hbm, st_hbm, gi_ref, gt_ref,
    ti_ref, si_ref, tt_ref, st_ref,
    it, is_, xt, xs, es, et, w, ist,
    row_acc, col_acc, row_inv, col_inv,
    isum, isum_in, tsum, tsum_sib, csum, tsum_in,
    di_keep, di_out, di_in, dt_keep, dt_other, dt_sib, dt_out, dt_in,
    in_sems, hop_send, hop_recv, sib_send, sib_recv, sum_send, sum_recv,
    grad_send, grad_recv, grad_sib_send, grad_sib_recv,
):
    grp, row, col = lax.axis_index("grp"), lax.axis_index("row"), lax.axis_index("col")
    x_hi, z = col // 4, lax.rem(col, 4)
    y, core = row // 2, lax.rem(row, 2)

    def image_peer(step, side):
        to_grp = 1 - grp if side else grp
        return (to_grp, lax.rem(y + step, 4) * 2 + core, col)

    def text_peer(step, side):
        to_grp = 1 - grp if side else grp
        to_hi = 1 - x_hi if side else x_hi
        return (to_grp, row, to_hi * 4 + lax.rem(z + step, 4))

    peers = (image_peer, text_peer)
    sibling = (grp, y * 2 + 1 - core, col)
    started = []

    def go(copy):
        copy.start()
        started.append(copy)

    def remote(src, dst, send, recv, device):
        return pltpu.make_async_remote_copy(
            src_ref=src, dst_ref=dst, send_sem=send, recv_sem=recv, device_id=device, device_id_type=MESH
        )

    barrier = pltpu.get_barrier_semaphore()
    for peer in peers:
        for to in (PAIR, PLUS, MINUS):
            pl.semaphore_signal(barrier, inc=1, device_id=peer(*to), device_id_type=MESH)
    pl.semaphore_signal(barrier, inc=1, device_id=sibling, device_id_type=MESH)

    loads = [
        pltpu.make_async_copy(src, dst, in_sems.at[i])
        for i, (src, dst) in enumerate(((si_hbm, si_ref), (st_hbm, st_ref), (ti_hbm, ti_ref), (tt_hbm, tt_ref)))
    ]
    for load in loads:
        load.start()
    i0, t0 = POS[0] * B, 2 * POS[0] * B
    for load, raw, out, at in zip(loads, (si_ref, st_ref, ti_ref, tt_ref), (is_, xs, it, xt), (i0, t0, i0, t0)):
        load.wait()
        out[at : at + B, :] = unit_rows(raw[...])[0].astype(BF16)

    arrays = ((it, is_, 1), (xt, xs, 2))

    def piece_ref(side, slot, piece):
        teach, stud, stride = arrays[side]
        first, rows = PIECE_ROWS[piece]
        ref = teach if piece[0] == "T" else stud
        return ref.at[pl.ds(POS[slot] * stride * B + first, rows), :]

    def hop(side, i):
        src, dst, to, piece = HOPS[i]
        return remote(
            piece_ref(side, src, piece), piece_ref(side, dst, piece),
            hop_send.at[side, i], hop_recv.at[side, i], peers[side](*to),
        )

    def index(dst, piece):
        return next(i for i, h in enumerate(HOPS) if h[1] == dst and h[3] == piece)

    def send(*names):
        for dst, piece in names:
            for side in (0, 1):
                go(hop(side, index(dst, piece)))

    def arrived(*names):
        for dst, piece in names:
            for side in (0, 1):
                hop(side, index(dst, piece)).wait_recv()

    def to_sibling(slot, kind):
        ref = xt if kind == "T" else xs
        k = 0 if kind == "T" else 1
        return remote(
            ref.at[pl.ds(2 * POS[slot] * B, B), :], ref.at[pl.ds((2 * POS[slot] + 1) * B, B), :],
            sib_send.at[k, slot], sib_recv.at[k, slot], sibling,
        )

    def share(kind, *slots):
        for slot in slots:
            go(to_sibling(slot, kind))

    def shared(kind, *slots):
        for slot in slots:
            to_sibling(slot, kind).wait_recv()

    def logits(mat, rows, cols):
        left, right, out = ((is_, xs, es), (it, xt, et))[mat]
        for c in range(cols[0] * 2 * B, cols[1] * 2 * B, 2 * B):
            r = rows[0] * B
            while r < rows[1] * B:
                n = min(512, rows[1] * B - r)
                e = jnp.exp2(dot_nt(left[r : r + n, :], right[c : c + 256, :]) * (LOGIT_SCALE * LOG2E))
                out[r : r + n, c : c + 256] = e
                row_acc[mat, r : r + n, :] += e[:, 0:128] + e[:, 128:256]
                col_acc[mat, :, c : c + 256] += jnp.sum(e.reshape(n // 8, 8, 256), axis=0)
                r += n

    pl.semaphore_wait(barrier, 7)

    send((1, "S"), (3, "T0"), (2, "T0"), (1, "T0"), (3, "T1"), (2, "T1"), (3, "S"), (2, "S"))
    share("T", 0)
    share("S", 0)

    row_acc[...] = jnp.zeros_like(row_acc)
    col_acc[...] = jnp.zeros_like(col_acc)

    arrived((3, "T0"))
    send((6, "T0"), (4, "T0"))
    arrived((1, "S"))
    share("S", 1)
    arrived((2, "T0"), (2, "T1"))
    send((5, "T1"), (4, "T1"), (1, "T1"))
    arrived((3, "T1"))
    send((6, "T1"), (5, "T0"), (6, "S"), (5, "S"))
    share("T", 2, 3)
    arrived((1, "T0"), (2, "S"), (3, "S"))
    send((4, "S0"), (4, "S1"))
    share("S", 2, 3)
    arrived((6, "T0"))
    send((7, "T0"))
    arrived((4, "T0"), (4, "T1"))
    share("T", 4)
    arrived((5, "T1"))
    send((7, "T1"))
    shared("T", 0, 2, 3, 4)
    logits(1, (0, 4), (0, 4))
    arrived((6, "S"), (5, "S"))
    send((7, "S0"), (7, "S1"))
    share("S", 6, 5)
    arrived((1, "T1"))
    share("T", 1)
    arrived((4, "S0"), (4, "S1"))
    share("S", 4)
    for s in (0, 1, 2, 3, 4, 5, 6):
        p = POS[s]
        ist[:, p * B : (p + 1) * B] = is_[p * B : (p + 1) * B, :].T
    shared("S", 0, 1, 2, 3, 4, 5, 6)
    logits(0, (0, 6), (0, 6))
    arrived((6, "T1"))
    share("T", 6)
    shared("T", 1, 6)
    logits(1, (4, 6), (0, 6))
    logits(1, (0, 4), (4, 6))
    arrived((7, "T0"), (7, "T1"), (5, "T0"))
    share("T", 7, 5)
    arrived((7, "S0"), (7, "S1"))
    share("S", 7)
    logits(1, (6, 8), (0, 6))
    logits(0, (6, 8), (0, 6))
    p = POS[7]
    ist[:, p * B : (p + 1) * B] = is_[p * B : (p + 1) * B, :].T
    shared("T", 7, 5)
    shared("S", 7)
    logits(1, (0, 8), (6, 8))
    logits(0, (0, 8), (6, 8))

    for mat in (0, 1):
        for b in range(2 * N):
            r = mat * 16 + b
            tsum[r : r + 1, :] = jnp.sum(col_acc[mat, :, b * B : (b + 1) * B], axis=0, keepdims=True)
    tsum_to_sib = remote(tsum, tsum_sib, sum_send.at[14], sum_recv.at[14], sibling)
    go(tsum_to_sib)
    for mat in (0, 1):
        for p in range(N):
            part = row_acc[mat, p * B : (p + 1) * B, :]
            isum[mat * N + p : mat * N + p + 1, :] = jnp.sum(part.T, axis=0, keepdims=True)

    def sum_copy(side, slot):
        back = minus(0, slot) - 1
        return remote(
            (isum, csum)[side], (isum_in, tsum_in)[side].at[back],
            sum_send.at[side * 7 + slot - 1], sum_recv.at[side * 7 + back], peers[side](*SLOTS[slot]),
        )

    def sum_from(side, slot):
        return remote(
            (isum, csum)[side], (isum_in, tsum_in)[side].at[slot - 1],
            sum_send.at[side * 7 + slot - 1], sum_recv.at[side * 7 + slot - 1], peers[side](*SLOTS[slot]),
        )

    for slot in range(N - 1, 0, -1):
        go(sum_copy(0, slot))
    tsum_to_sib.wait_recv()
    for mat in (0, 1):
        for p in range(N):
            r = mat * 16 + 2 * p
            csum[r : r + 1, :] = tsum[r : r + 1, :] + tsum_sib[r + 1 : r + 2, :]
            csum[r + 1 : r + 2, :] = tsum[r + 1 : r + 2, :] + tsum_sib[r : r + 1, :]
    for slot in range(N - 1, 0, -1):
        go(sum_copy(1, slot))

    half = 0.5 * LOGIT_SCALE
    for slot in range(1, N):
        sum_from(0, slot).wait_recv()
    for mat in (0, 1):
        for t in range(N):
            r = mat * N + POS[t]
            total = isum[r : r + 1, :]
            for e in range(1, N):
                q = mat * N + POS[minus(t, e)]
                total = total + isum_in[e - 1, q : q + 1, :]
            row_inv[mat, POS[t] * B : (POS[t] + 1) * B, :] = jnp.broadcast_to(half / total, (B, B)).T
    for slot in range(1, N):
        sum_from(1, slot).wait_recv()
    for mat in (0, 1):
        for t in range(N):
            for par in (0, 1):
                r = mat * 16 + 2 * POS[t] + par
                total = csum[r : r + 1, :]
                for e in range(1, N):
                    q = mat * 16 + 2 * POS[minus(t, e)] + par
                    total = total + tsum_in[e - 1, q : q + 1, :]
                c = (2 * POS[t] + par) * B
                col_inv[mat, :, c : c + B] = jnp.broadcast_to(half / total, (8, B))

    def weights(rows, cols):
        for r in range(rows[0] * B, rows[1] * B, 64):
            for c in range(cols[0] * 2 * B, cols[1] * 2 * B, B):
                terms = []
                for mat, e in ((0, es), (1, et)):
                    factor = row_inv[mat, r : r + 64, :].reshape(8, 8, B) + col_inv[mat, :, c : c + B][None]
                    terms.append(e[r : r + 64, c : c + B].reshape(8, 8, B) * factor)
                w[r : r + 64, c : c + B] = (terms[0] - terms[1]).reshape(64, B).astype(BF16)

    def grad_copy(side, slot):
        return remote(
            (di_out, dt_out)[side].at[slot], (di_in, dt_in)[side].at[slot],
            grad_send.at[side, slot], grad_recv.at[side, slot], peers[side](*GRAD_TO[slot]),
        )

    def grad_sib(slot):
        return remote(
            dt_other.at[slot], dt_sib.at[slot], grad_sib_send.at[slot], grad_sib_recv.at[slot], sibling
        )

    def text_terms(*slots):
        for slot in slots:
            c = 2 * POS[slot] * B
            out = jnp.dot(ist[...], w[:, c : c + 2 * B], preferred_element_type=F32)
            dt_keep[slot] = out[:, 0:B]
            dt_other[slot] = out[:, B : 2 * B].astype(BF16)
            go(grad_sib(slot))

    def total_of(side, slot):
        if side == 0:
            total = di_keep[slot]
        else:
            grad_sib(slot).wait_recv()
            total = dt_keep[slot] + dt_sib[slot].astype(F32)
        for source in SINKS.get(slot, ()):
            grad_copy(side, source).wait_recv()
            total = total + (di_in, dt_in)[side][source].astype(F32)
        return total

    def grad_send_from(side, *slots):
        for slot in slots:
            (di_out, dt_out)[side][slot] = total_of(side, slot).astype(BF16)
            go(grad_copy(side, slot))

    def image_terms(p0, p1):
        out = jnp.dot(w[p0 * B : p1 * B, :], xs[...], preferred_element_type=F32)
        for p in range(p0, p1):
            part = out[(p - p0) * B : (p - p0 + 1) * B, :]
            if ORDER[p] in SINKS:
                di_keep[ORDER[p]] = part
            else:
                di_out[ORDER[p]] = part.astype(BF16)
        for p in range(p1 - 1, p0 - 1, -1):
            if ORDER[p] not in SINKS:
                go(grad_copy(0, ORDER[p]))

    weights((0, 8), (5, 8))
    text_terms(7, 5, 6)
    weights((5, 8), (0, 5))
    image_terms(5, 8)
    grad_send_from(1, 7, 5, 6)
    weights((0, 5), (0, 5))
    text_terms(2, 3)
    image_terms(0, 2)
    grad_send_from(1, 2, 3)
    text_terms(4, 1, 0)
    image_terms(2, 5)
    grad_send_from(0, 4, 1)
    grad_send_from(1, 4, 1)

    def finish(raw, total):
        norm, inverse = unit_rows(raw)
        return inverse * (total - norm * jnp.sum(norm * total, axis=1, keepdims=True))

    gi_ref[...] = finish(si_ref[...], total_of(0, 0))
    gt_ref[...] = finish(st_ref[...], total_of(1, 0).T)

    for copy in started:
        copy.wait_send()


def per_device(teacher_image, student_image, teacher_text, student_text):
    vmem, anywhere = pl.BlockSpec(memory_space=pltpu.VMEM), pl.BlockSpec(memory_space=pl.ANY)
    dma = pltpu.SemaphoreType.DMA
    return pl.pallas_call(
        kernel,
        out_shape=(jax.ShapeDtypeStruct((B, 512), F32), jax.ShapeDtypeStruct((B, 512), F32)),
        in_specs=[anywhere] * 4,
        out_specs=(vmem, vmem),
        scratch_shapes=[
            pltpu.VMEM((B, 1024), BF16),
            pltpu.VMEM((B, 512), BF16),
            pltpu.VMEM((B, 1024), BF16),
            pltpu.VMEM((B, 512), BF16),
            pltpu.VMEM((N * B, 1024), BF16),
            pltpu.VMEM((N * B, 512), BF16),
            pltpu.VMEM((2 * N * B, 1024), BF16),
            pltpu.VMEM((2 * N * B, 512), BF16),
            pltpu.VMEM((N * B, 2 * N * B), F32),
            pltpu.VMEM((N * B, 2 * N * B), F32),
            pltpu.VMEM((N * B, 2 * N * B), BF16),
            pltpu.VMEM((512, N * B), BF16),
            pltpu.VMEM((2, N * B, B), F32),
            pltpu.VMEM((2, 8, 2 * N * B), F32),
            pltpu.VMEM((2, N * B, B), F32),
            pltpu.VMEM((2, 8, 2 * N * B), F32),
            pltpu.VMEM((16, B), F32),
            pltpu.VMEM((7, 16, B), F32),
            pltpu.VMEM((32, B), F32),
            pltpu.VMEM((32, B), F32),
            pltpu.VMEM((32, B), F32),
            pltpu.VMEM((7, 32, B), F32),
            pltpu.VMEM((N, B, 512), F32),
            pltpu.VMEM((N, B, 512), BF16),
            pltpu.VMEM((N, B, 512), BF16),
            pltpu.VMEM((N, 512, B), F32),
            pltpu.VMEM((N, 512, B), BF16),
            pltpu.VMEM((N, 512, B), BF16),
            pltpu.VMEM((N, 512, B), BF16),
            pltpu.VMEM((N, 512, B), BF16),
            dma((4,)),
            dma((2, N_HOPS)),
            dma((2, N_HOPS)),
            dma((2, N)),
            dma((2, N)),
            dma((15,)),
            dma((15,)),
            dma((2, N)),
            dma((2, N)),
            dma((N,)),
            dma((N,)),
        ],
        compiler_params=pltpu.CompilerParams(
            collective_id=0, has_side_effects=True, vmem_limit_bytes=60 << 20
        ),
        cost_estimate=pl.CostEstimate(flops=10_737_418_240, bytes_accessed=1 << 20, transcendentals=1 << 22),
    )(teacher_image, student_image, teacher_text, student_text)


def solution(mesh):
    spec = P(("grp", "row", "col"), None)
    return jax.shard_map(
        per_device, mesh=mesh, in_specs=(spec,) * 4, out_specs=(spec, spec), check_vma=False
    )
```

time: 553 us -> 63.6 us (0.12)
  waiting for transfers between devices: 363 us -> 0 us
  blocking collectives: 96.6 us -> 0 us
  Pallas kernels: 0 us -> 60.4 us
  matrix products: 49.9 us -> 0 us
  other arithmetic: 25.7 us -> 0 us
  between operations: 14.3 us -> 0.65 us
    all_gather x4 -> x0, waiting for transfers between devices: 193 us -> none  [the longest x1 79 us: per_device(): lax.all_gather(teacher_image, ('grp', 'col'), axis=0, tiled=True)]
    psum x2 -> x0, waiting for transfers between devices: 168 us -> none  [the longest x1 105 us: per_device(): full_image = lax.psum(image_terms, ('grp', 'col'))]
    psum x2 -> x0, blocking collectives: 96.6 us -> none  [the longest x1 60 us: per_device(): lax.psum((row_student, row_teacher), ('grp', 'col'))]
    pallas_call x0 -> x1, Pallas kernels: none -> 60.4 us  [per_device(): pl.pallas_call(kernel, out_shape=(jax.ShapeDtypeStruct((B, 512), F32), ja...]
    dot_general x24 -> x0, matrix products: 49.9 us -> none  [the longest x16 39.4 us: logits(): jnp.dot(left, right.T, preferred_element_type=jnp.float32)]
    reduce_sum x6 -> x0, other arithmetic: 11.4 us -> none  [the longest x4 9.16 us: unit_rows(): inverse = lax.rsqrt(jnp.sum(values * values, axis=1, keepdims=True) + EPS)]
    convert_element_type x3 -> x0, other arithmetic: 7.59 us -> none  [the longest x1 3.13 us: per_device(): unit_si = norm_si.astype(jnp.bfloat16)]
    mul x3 -> x0, other arithmetic: 6.6 us -> none  [the longest x1 2.91 us: unit_rows(): return (values * inverse, inverse)]
  transfers between devices with their start and end apart: 6 -> 0, of which waited for: 6 -> 0; matrix products, arithmetic and copies ran while one was open for 3% -> 0% of each run, Pallas kernels for 0% -> 0%
where the time goes in v2:
time: 63.6 us; the launch traced here: 63.5 us
  Pallas kernels  60.4 us (95%)
  local copies, waits for them, and re-layouts  2.42 us (4%)
  between operations  0.65 us (1%)
    pallas_call x1, Pallas kernels, per_device(): pl.pallas_call(kernel, out_shape=(jax.ShapeDtypeStruct((B, 512), F32), ja...  60.4 us
    unnamed x4, local copies, waits for them, and re-layouts  2.42 us

profile of v2, /device:TPU:1, one launch (start us, length us, event | category | flops | bytes accessed | tf_op | source)
XLA Modules:
  0.0 63.5 jit_solution(3951309277195675250)
XLA Ops:
  0.6 60.4 %shard_map.59 = (f32[128,512]{1,0:T(8,128)}, f32[128,512]{1,0:T(8,128)}) custom-call(bf16[128,1024]{1,0:T(8,128)(2,1)} %ti_hbm.1, bf16[128,512]{1,0:T(8,128)(2,1)} %si_hbm.1, bf16[128,1024]{1,0:T(8,128)(2,1)} %tt_hbm.1, bf16[128,512]{1,0:T(8,128)(2,1)} %st_hbm.1), custom_call_target="tpu_custom_call" | custom-call | flops 10737418240 | bytes 1048576 | tf_op jit(solution)/shard_map/pallas_call | solution.py:382
  61.0 0.0 copy-start
  61.0 1.7 %copy.8 = f32[128,512]{1,0:T(8,128)} copy(f32[128,512]{1,0:T(8,128)} %get-tuple-element.4) | data formatting | bytes 524288
  62.8 0.0 copy-done
  62.8 0.7 %copy.9 = f32[128,512]{1,0:T(8,128)} copy(f32[128,512]{1,0:T(8,128)S(1)} %copy-done) | data formatting | bytes 524288
Async XLA Ops:
  61.0 1.7 %copy-start = (f32[128,512]{1,0:T(8,128)S(1)}, f32[128,512]{1,0:T(8,128)}, u32[]{:S(2)}) copy-start(f32[128,512]{1,0:T(8,128)} %get-tuple-element.5) | copy-start | bytes 786436

commit v3 on v2

--- a/solution.py
+++ b/solution.py
@@ -14,7 +14,7 @@
 
 SLOTS = [(0, 0), (0, 1), (1, 0), (3, 0), (2, 0), (1, 1), (3, 1), (2, 1)]
 N = len(SLOTS)
-ORDER = [2, 3, 4, 0, 1, 6, 5, 7]
+ORDER = [0, 2, 3, 4, 5, 6, 1, 7]
 POS = [ORDER.index(s) for s in range(N)]
 
 
@@ -40,22 +40,20 @@
     (3, 4, PLUS, "T0"),
     (2, 5, PAIR, "T1"),
     (2, 4, MINUS, "T1"),
+    (3, 6, PAIR, "T1"),
     (0, 1, PAIR, "T1"),
-    (3, 6, PAIR, "T1"),
-    (2, 5, PAIR, "T0"),
+    (1, 5, MINUS, "T0"),
+    (1, 5, MINUS, "S"),
+    (3, 4, PLUS, "S"),
     (1, 6, PLUS, "S"),
-    (1, 5, MINUS, "S"),
-    (3, 4, PLUS, "S0"),
-    (2, 4, MINUS, "S1"),
     (6, 7, PLUS, "T0"),
     (5, 7, MINUS, "T1"),
-    (6, 7, PLUS, "S0"),
-    (5, 7, MINUS, "S1"),
+    (4, 7, PAIR, "S"),
 ]
-PIECE_ROWS = {"T0": (0, 64), "T1": (64, 64), "S": (0, 128), "S0": (0, 64), "S1": (64, 64)}
+PIECE_ROWS = {"T0": (0, 64), "T1": (64, 64), "S": (0, 128)}
 N_HOPS = len(HOPS)
 GRAD_TO = {7: PAIR, 5: PLUS, 6: MINUS, 2: PLUS, 3: MINUS, 4: ACROSS, 1: PAIR}
-SINKS = {4: (7,), 1: (5, 6), 0: (2, 3, 4, 1)}
+SINKS = {4: (7,), 1: (5, 6), 0: (2, 3, 1, 4)}
 
 
 def dot_nt(a, b):
@@ -95,6 +93,9 @@
     sibling = (grp, y * 2 + 1 - core, col)
     started = []
 
+    def segment(work):
+        pl.when(grp >= 0)(work)
+
     def go(copy):
         copy.start()
         started.append(copy)
@@ -183,69 +184,119 @@
     share("T", 0)
     share("S", 0)
 
-    row_acc[...] = jnp.zeros_like(row_acc)
-    col_acc[...] = jnp.zeros_like(col_acc)
+    @segment
+    def _():
+        row_acc[...] = jnp.zeros_like(row_acc)
+        col_acc[...] = jnp.zeros_like(col_acc)
 
     arrived((3, "T0"))
     send((6, "T0"), (4, "T0"))
     arrived((1, "S"))
     share("S", 1)
     arrived((2, "T0"), (2, "T1"))
-    send((5, "T1"), (4, "T1"), (1, "T1"))
+    send((5, "T1"), (4, "T1"))
     arrived((3, "T1"))
-    send((6, "T1"), (5, "T0"), (6, "S"), (5, "S"))
+    send((6, "T1"), (1, "T1"))
+    arrived((1, "T0"))
+    send((5, "T0"), (5, "S"))
     share("T", 2, 3)
-    arrived((1, "T0"), (2, "S"), (3, "S"))
-    send((4, "S0"), (4, "S1"))
+    arrived((3, "S"))
+    send((4, "S"), (6, "S"))
+    arrived((2, "S"))
     share("S", 2, 3)
     arrived((6, "T0"))
     send((7, "T0"))
+    shared("T", 0, 2, 3)
+
+    @segment
+    def _():
+        logits(1, (0, 3), (0, 3))
+
+    shared("S", 0, 1, 2, 3)
+
+    @segment
+    def _():
+        logits(0, (0, 3), (0, 3))
+        logits(0, (0, 3), (6, 7))
+
     arrived((4, "T0"), (4, "T1"))
     share("T", 4)
     arrived((5, "T1"))
     send((7, "T1"))
-    shared("T", 0, 2, 3, 4)
-    logits(1, (0, 4), (0, 4))
-    arrived((6, "S"), (5, "S"))
-    send((7, "S0"), (7, "S1"))
-    share("S", 6, 5)
+    arrived((4, "S"))
+    send((7, "S"))
+    share("S", 4)
+    arrived((5, "T0"), (6, "T1"))
+    share("T", 5, 6)
+    shared("T", 4)
+
+    @segment
+    def _():
+        logits(1, (0, 3), (3, 4))
+        logits(1, (3, 6), (0, 4))
+
+    shared("T", 5, 6)
+
+    @segment
+    def _():
+        logits(1, (0, 6), (4, 6))
+
+    arrived((5, "S"), (6, "S"))
+    share("S", 5, 6)
     arrived((1, "T1"))
     share("T", 1)
-    arrived((4, "S0"), (4, "S1"))
-    share("S", 4)
-    for s in (0, 1, 2, 3, 4, 5, 6):
-        p = POS[s]
-        ist[:, p * B : (p + 1) * B] = is_[p * B : (p + 1) * B, :].T
-    shared("S", 0, 1, 2, 3, 4, 5, 6)
-    logits(0, (0, 6), (0, 6))
-    arrived((6, "T1"))
-    share("T", 6)
-    shared("T", 1, 6)
-    logits(1, (4, 6), (0, 6))
-    logits(1, (0, 4), (4, 6))
-    arrived((7, "T0"), (7, "T1"), (5, "T0"))
-    share("T", 7, 5)
-    arrived((7, "S0"), (7, "S1"))
+
+    @segment
+    def _():
+        logits(0, (3, 6), (0, 3))
+        logits(0, (3, 6), (6, 7))
+
+    shared("S", 4, 5, 6)
+
+    @segment
+    def _():
+        logits(0, (0, 6), (3, 6))
+
+    shared("T", 1)
+
+    @segment
+    def _():
+        logits(1, (0, 6), (6, 7))
+
+    arrived((7, "T0"), (7, "T1"))
+    share("T", 7)
+    arrived((7, "S"))
     share("S", 7)
-    logits(1, (6, 8), (0, 6))
-    logits(0, (6, 8), (0, 6))
-    p = POS[7]
-    ist[:, p * B : (p + 1) * B] = is_[p * B : (p + 1) * B, :].T
-    shared("T", 7, 5)
+
+    @segment
+    def _():
+        logits(1, (6, 8), (0, 7))
+        logits(0, (6, 8), (0, 7))
+
+    shared("T", 7)
     shared("S", 7)
-    logits(1, (0, 8), (6, 8))
-    logits(0, (0, 8), (6, 8))
-
-    for mat in (0, 1):
-        for b in range(2 * N):
-            r = mat * 16 + b
-            tsum[r : r + 1, :] = jnp.sum(col_acc[mat, :, b * B : (b + 1) * B], axis=0, keepdims=True)
+
+    @segment
+    def _():
+        logits(1, (0, 8), (7, 8))
+        logits(0, (0, 8), (7, 8))
+
+    @segment
+    def _():
+        for mat in (0, 1):
+            for b in range(2 * N):
+                r = mat * 16 + b
+                tsum[r : r + 1, :] = jnp.sum(col_acc[mat, :, b * B : (b + 1) * B], axis=0, keepdims=True)
+
     tsum_to_sib = remote(tsum, tsum_sib, sum_send.at[14], sum_recv.at[14], sibling)
     go(tsum_to_sib)
-    for mat in (0, 1):
-        for p in range(N):
-            part = row_acc[mat, p * B : (p + 1) * B, :]
-            isum[mat * N + p : mat * N + p + 1, :] = jnp.sum(part.T, axis=0, keepdims=True)
+
+    @segment
+    def _():
+        for mat in (0, 1):
+            for p in range(N):
+                part = row_acc[mat, p * B : (p + 1) * B, :]
+                isum[mat * N + p : mat * N + p + 1, :] = jnp.sum(part.T, axis=0, keepdims=True)
 
     def sum_copy(side, slot):
         back = minus(0, slot) - 1
@@ -270,6 +321,11 @@
             csum[r + 1 : r + 2, :] = tsum[r + 1 : r + 2, :] + tsum_sib[r : r + 1, :]
     for slot in range(N - 1, 0, -1):
         go(sum_copy(1, slot))
+
+    @segment
+    def _():
+        for p in range(N):
+            ist[:, p * B : (p + 1) * B] = is_[p * B : (p + 1) * B, :].T
 
     half = 0.5 * LOGIT_SCALE
     for slot in range(1, N):
@@ -321,6 +377,9 @@
             out = jnp.dot(ist[...], w[:, c : c + 2 * B], preferred_element_type=F32)
             dt_keep[slot] = out[:, 0:B]
             dt_other[slot] = out[:, B : 2 * B].astype(BF16)
+
+    def text_share(*slots):
+        for slot in slots:
             go(grad_sib(slot))
 
     def total_of(side, slot):
@@ -347,23 +406,67 @@
                 di_keep[ORDER[p]] = part
             else:
                 di_out[ORDER[p]] = part.astype(BF16)
-        for p in range(p1 - 1, p0 - 1, -1):
-            if ORDER[p] not in SINKS:
-                go(grad_copy(0, ORDER[p]))
-
-    weights((0, 8), (5, 8))
-    text_terms(7, 5, 6)
-    weights((5, 8), (0, 5))
-    image_terms(5, 8)
-    grad_send_from(1, 7, 5, 6)
-    weights((0, 5), (0, 5))
-    text_terms(2, 3)
-    image_terms(0, 2)
+
+    def image_send(*slots):
+        for slot in slots:
+            go(grad_copy(0, slot))
+
+    @segment
+    def _():
+        weights((0, 8), (7, 8))
+        text_terms(7)
+
+    text_share(7)
+
+    @segment
+    def _():
+        weights((0, 8), (4, 6))
+        text_terms(5, 6)
+
+    text_share(5, 6)
+
+    @segment
+    def _():
+        weights((6, 8), (0, 4))
+        weights((6, 8), (6, 7))
+        image_terms(6, 8)
+
+    image_send(7)
+    grad_send_from(1, 7)
+
+    @segment
+    def _():
+        weights((4, 6), (0, 4))
+        weights((4, 6), (6, 7))
+        image_terms(4, 6)
+
+    image_send(5, 6)
+    grad_send_from(1, 5, 6)
+
+    @segment
+    def _():
+        weights((0, 4), (0, 4))
+        text_terms(2, 3)
+
+    text_share(2, 3)
+
+    @segment
+    def _():
+        weights((0, 4), (6, 7))
+        image_terms(0, 4)
+
+    image_send(2, 3)
     grad_send_from(1, 2, 3)
-    text_terms(4, 1, 0)
-    image_terms(2, 5)
-    grad_send_from(0, 4, 1)
-    grad_send_from(1, 4, 1)
+
+    @segment
+    def _():
+        text_terms(4, 1, 0)
+
+    text_share(4, 1, 0)
+    grad_send_from(0, 4)
+    grad_send_from(1, 4)
+    grad_send_from(0, 1)
+    grad_send_from(1, 1)
 
     def finish(raw, total):
         norm, inverse = unit_rows(raw)

time: 63.6 us -> 59 us (0.928)
  Pallas kernels: 60.4 us -> 55.8 us
    pallas_call x1, Pallas kernels: 60.4 us -> 55.8 us  [per_device(): pl.pallas_call(kernel, out_shape=(jax.ShapeDtypeStruct((B, 512), F32), ja...]
where the time goes in v3:
time: 59 us; the launch traced here: 58.9 us
  Pallas kernels  55.8 us (95%)
  local copies, waits for them, and re-layouts  2.42 us (4%)
  between operations  0.65 us (1%)
    pallas_call x1, Pallas kernels, per_device(): pl.pallas_call(kernel, out_shape=(jax.ShapeDtypeStruct((B, 512), F32), ja...  55.8 us
    unnamed x4, local copies, waits for them, and re-layouts  2.42 us

profile of v3, /device:TPU:1, one launch (start us, length us, event | category | flops | bytes accessed | tf_op | source)
XLA Modules:
  0.0 58.9 jit_solution(15041944335174061729)
XLA Ops:
  0.6 55.8 %shard_map.59 = (f32[128,512]{1,0:T(8,128)}, f32[128,512]{1,0:T(8,128)}) custom-call(bf16[128,1024]{1,0:T(8,128)(2,1)} %ti_hbm.1, bf16[128,512]{1,0:T(8,128)(2,1)} %si_hbm.1, bf16[128,1024]{1,0:T(8,128)(2,1)} %tt_hbm.1, bf16[128,512]{1,0:T(8,128)(2,1)} %st_hbm.1), custom_call_target="tpu_custom_call" | custom-call | flops 10737418240 | bytes 1048576 | tf_op jit(solution)/shard_map/pallas_call | solution.py:485
  56.5 0.0 copy-start
  56.5 1.7 %copy.8 = f32[128,512]{1,0:T(8,128)} copy(f32[128,512]{1,0:T(8,128)} %get-tuple-element.4) | data formatting | bytes 524288
  58.2 0.0 copy-done
  58.2 0.7 %copy.9 = f32[128,512]{1,0:T(8,128)} copy(f32[128,512]{1,0:T(8,128)S(1)} %copy-done) | data formatting | bytes 524288
Async XLA Ops:
  56.5 1.7 %copy-start = (f32[128,512]{1,0:T(8,128)S(1)}, f32[128,512]{1,0:T(8,128)}, u32[]{:S(2)}) copy-start(f32[128,512]{1,0:T(8,128)} %get-tuple-element.5) | copy-start | bytes 786436

commit v4 on v3

--- a/solution.py
+++ b/solution.py
@@ -14,7 +14,7 @@
 
 SLOTS = [(0, 0), (0, 1), (1, 0), (3, 0), (2, 0), (1, 1), (3, 1), (2, 1)]
 N = len(SLOTS)
-ORDER = [0, 2, 3, 4, 5, 6, 1, 7]
+ORDER = [0, 2, 3, 4, 1, 7, 5, 6]
 POS = [ORDER.index(s) for s in range(N)]
 
 
@@ -54,6 +54,7 @@
 N_HOPS = len(HOPS)
 GRAD_TO = {7: PAIR, 5: PLUS, 6: MINUS, 2: PLUS, 3: MINUS, 4: ACROSS, 1: PAIR}
 SINKS = {4: (7,), 1: (5, 6), 0: (2, 3, 1, 4)}
+HALVED = ()
 
 
 def dot_nt(a, b):
@@ -118,9 +119,9 @@
     for load in loads:
         load.start()
     i0, t0 = POS[0] * B, 2 * POS[0] * B
-    for load, raw, out, at in zip(loads, (si_ref, st_ref, ti_ref, tt_ref), (is_, xs, it, xt), (i0, t0, i0, t0)):
-        load.wait()
-        out[at : at + B, :] = unit_rows(raw[...])[0].astype(BF16)
+
+    def normalize(raw, out, at, first, rows):
+        out[at + first : at + first + rows, :] = unit_rows(raw[first : first + rows, :])[0].astype(BF16)
 
     arrays = ((it, is_, 1), (xt, xs, 2))
 
@@ -145,9 +146,9 @@
             for side in (0, 1):
                 go(hop(side, index(dst, piece)))
 
-    def arrived(*names):
+    def arrived(*names, sides=(0, 1)):
         for dst, piece in names:
-            for side in (0, 1):
+            for side in sides:
                 hop(side, index(dst, piece)).wait_recv()
 
     def to_sibling(slot, kind):
@@ -178,9 +179,28 @@
                 col_acc[mat, :, c : c + 256] += jnp.sum(e.reshape(n // 8, 8, 256), axis=0)
                 r += n
 
+    loads[0].wait()
+    loads[1].wait()
+    normalize(si_ref, is_, i0, 0, B)
+    normalize(st_ref, xs, t0, 0, B)
     pl.semaphore_wait(barrier, 7)
-
-    send((1, "S"), (3, "T0"), (2, "T0"), (1, "T0"), (3, "T1"), (2, "T1"), (3, "S"), (2, "S"))
+    send((1, "S"))
+    loads[2].wait()
+    loads[3].wait()
+
+    @segment
+    def _():
+        normalize(ti_ref, it, i0, 0, 64)
+        normalize(tt_ref, xt, t0, 0, 64)
+
+    send((3, "T0"), (2, "T0"), (1, "T0"))
+
+    @segment
+    def _():
+        normalize(ti_ref, it, i0, 64, 64)
+        normalize(tt_ref, xt, t0, 64, 64)
+
+    send((3, "T1"), (2, "T1"), (3, "S"), (2, "S"))
     share("T", 0)
     share("S", 0)
 
@@ -198,172 +218,211 @@
     arrived((3, "T1"))
     send((6, "T1"), (1, "T1"))
     arrived((1, "T0"))
-    send((5, "T0"), (5, "S"))
+    send((5, "T0"))
     share("T", 2, 3)
     arrived((3, "S"))
-    send((4, "S"), (6, "S"))
+    send((4, "S"))
     arrived((2, "S"))
     share("S", 2, 3)
     arrived((6, "T0"))
-    send((7, "T0"))
+    send((7, "T0"), (6, "S"))
     shared("T", 0, 2, 3)
 
     @segment
     def _():
         logits(1, (0, 3), (0, 3))
-
-    shared("S", 0, 1, 2, 3)
-
-    @segment
-    def _():
-        logits(0, (0, 3), (0, 3))
-        logits(0, (0, 3), (6, 7))
 
     arrived((4, "T0"), (4, "T1"))
     share("T", 4)
     arrived((5, "T1"))
-    send((7, "T1"))
+    send((7, "T1"), (5, "S"))
+    shared("S", 0, 1, 2, 3)
+
+    @segment
+    def _():
+        logits(0, (0, 3), (0, 3))
+        logits(0, (0, 3), (4, 5))
+
+    shared("T", 4)
+
+    @segment
+    def _():
+        logits(1, (0, 3), (3, 4))
+        logits(1, (3, 4), (0, 4))
+
     arrived((4, "S"))
     send((7, "S"))
     share("S", 4)
     arrived((5, "T0"), (6, "T1"))
     share("T", 5, 6)
-    shared("T", 4)
-
-    @segment
-    def _():
-        logits(1, (0, 3), (3, 4))
-        logits(1, (3, 6), (0, 4))
+
+    @segment
+    def _():
+        logits(1, (6, 8), (0, 4))
 
     shared("T", 5, 6)
 
     @segment
     def _():
-        logits(1, (0, 6), (4, 6))
-
-    arrived((5, "S"), (6, "S"))
-    share("S", 5, 6)
-    arrived((1, "T1"))
-    share("T", 1)
-
-    @segment
-    def _():
-        logits(0, (3, 6), (0, 3))
-        logits(0, (3, 6), (6, 7))
-
-    shared("S", 4, 5, 6)
-
-    @segment
-    def _():
-        logits(0, (0, 6), (3, 6))
-
-    shared("T", 1)
-
-    @segment
-    def _():
-        logits(1, (0, 6), (6, 7))
-
-    arrived((7, "T0"), (7, "T1"))
-    share("T", 7)
-    arrived((7, "S"))
-    share("S", 7)
-
-    @segment
-    def _():
-        logits(1, (6, 8), (0, 7))
-        logits(0, (6, 8), (0, 7))
-
-    shared("T", 7)
-    shared("S", 7)
-
-    @segment
-    def _():
-        logits(1, (0, 8), (7, 8))
-        logits(0, (0, 8), (7, 8))
-
-    @segment
-    def _():
-        for mat in (0, 1):
-            for b in range(2 * N):
-                r = mat * 16 + b
-                tsum[r : r + 1, :] = jnp.sum(col_acc[mat, :, b * B : (b + 1) * B], axis=0, keepdims=True)
-
-    tsum_to_sib = remote(tsum, tsum_sib, sum_send.at[14], sum_recv.at[14], sibling)
-    go(tsum_to_sib)
-
-    @segment
-    def _():
-        for mat in (0, 1):
-            for p in range(N):
-                part = row_acc[mat, p * B : (p + 1) * B, :]
-                isum[mat * N + p : mat * N + p + 1, :] = jnp.sum(part.T, axis=0, keepdims=True)
-
-    def sum_copy(side, slot):
+        logits(1, (0, 4), (6, 8))
+        logits(1, (6, 8), (6, 8))
+
+    for slot, pieces in ((1, ("T1",)), (7, ("T0", "T1"))):
+        arrived(*((slot, piece) for piece in pieces), sides=(1,))
+        share("T", slot)
+    arrived((1, "T1"), (7, "T0"), (7, "T1"), sides=(0,))
+    shared("S", 4)
+
+    @segment
+    def _():
+        logits(0, (3, 5), (0, 5))
+        logits(0, (0, 3), (3, 4))
+        logits(1, (4, 6), (0, 4))
+        logits(1, (4, 6), (6, 8))
+
+    shared("T", 1, 7)
+
+    @segment
+    def _():
+        logits(1, (0, 4), (4, 6))
+
+    for slot in (5, 6, 7):
+        arrived((slot, "S"), sides=(1,))
+        share("S", slot)
+
+    @segment
+    def _():
+        logits(1, (4, 8), (4, 6))
+
+    arrived((5, "S"), (6, "S"), (7, "S"), sides=(0,))
+
+    def sum_sib(mat):
+        return remote(tsum.at[mat], tsum_sib.at[mat], sum_send.at[mat, 14], sum_recv.at[mat, 14], sibling)
+
+    def sum_copy(mat, side, slot):
         back = minus(0, slot) - 1
         return remote(
-            (isum, csum)[side], (isum_in, tsum_in)[side].at[back],
-            sum_send.at[side * 7 + slot - 1], sum_recv.at[side * 7 + back], peers[side](*SLOTS[slot]),
+            (isum, csum)[side].at[mat], (isum_in, tsum_in)[side].at[mat, back],
+            sum_send.at[mat, side * 7 + slot - 1], sum_recv.at[mat, side * 7 + back], peers[side](*SLOTS[slot]),
         )
 
-    def sum_from(side, slot):
+    def sum_from(mat, side, slot):
         return remote(
-            (isum, csum)[side], (isum_in, tsum_in)[side].at[slot - 1],
-            sum_send.at[side * 7 + slot - 1], sum_recv.at[side * 7 + slot - 1], peers[side](*SLOTS[slot]),
+            (isum, csum)[side].at[mat], (isum_in, tsum_in)[side].at[mat, slot - 1],
+            sum_send.at[mat, side * 7 + slot - 1], sum_recv.at[mat, side * 7 + slot - 1], peers[side](*SLOTS[slot]),
         )
 
-    for slot in range(N - 1, 0, -1):
-        go(sum_copy(0, slot))
-    tsum_to_sib.wait_recv()
-    for mat in (0, 1):
-        for p in range(N):
-            r = mat * 16 + 2 * p
-            csum[r : r + 1, :] = tsum[r : r + 1, :] + tsum_sib[r + 1 : r + 2, :]
-            csum[r + 1 : r + 2, :] = tsum[r + 1 : r + 2, :] + tsum_sib[r : r + 1, :]
-    for slot in range(N - 1, 0, -1):
-        go(sum_copy(1, slot))
+    def sums_out(mat):
+        @segment
+        def _():
+            for b in range(2 * N):
+                tsum[mat, b : b + 1, :] = jnp.sum(col_acc[mat, :, b * B : (b + 1) * B], axis=0, keepdims=True)
+
+        go(sum_sib(mat))
+
+        @segment
+        def _():
+            for p in range(N):
+                isum[mat, p : p + 1, :] = jnp.sum(row_acc[mat, p * B : (p + 1) * B, :].T, axis=0, keepdims=True)
+
+        for slot in range(N - 1, 0, -1):
+            go(sum_copy(mat, 0, slot))
+
+    def text_sums_out(mat):
+        sum_sib(mat).wait_recv()
+
+        @segment
+        def _():
+            for p in range(N):
+                r = 2 * p
+                csum[mat, r : r + 1, :] = tsum[mat, r : r + 1, :] + tsum_sib[mat, r + 1 : r + 2, :]
+                csum[mat, r + 1 : r + 2, :] = tsum[mat, r + 1 : r + 2, :] + tsum_sib[mat, r : r + 1, :]
+
+        for slot in range(N - 1, 0, -1):
+            go(sum_copy(mat, 1, slot))
+
+    half = 0.5 * LOGIT_SCALE
+
+    def sums_in(mat):
+        for slot in range(1, N):
+            sum_from(mat, 0, slot).wait_recv()
+
+        @segment
+        def _():
+            for t in range(N):
+                total = isum[mat, POS[t] : POS[t] + 1, :]
+                for e in range(1, N):
+                    q = POS[minus(t, e)]
+                    total = total + isum_in[mat, e - 1, q : q + 1, :]
+                row_inv[mat, POS[t] * B : (POS[t] + 1) * B, :] = jnp.broadcast_to(half / total, (B, B)).T
+
+        for slot in range(1, N):
+            sum_from(mat, 1, slot).wait_recv()
+
+        @segment
+        def _():
+            for t in range(N):
+                for par in (0, 1):
+                    r = 2 * POS[t] + par
+                    total = csum[mat, r : r + 1, :]
+                    for e in range(1, N):
+                        q = 2 * POS[minus(t, e)] + par
+                        total = total + tsum_in[mat, e - 1, q : q + 1, :]
+                    col_inv[mat, :, r * B : (r + 1) * B] = jnp.broadcast_to(half / total, (8, B))
+
+    def weighted(mat, e, r, c):
+        factor = row_inv[mat, r : r + 64, :].reshape(8, 8, B) + col_inv[mat, :, c : c + B][None]
+        return e[r : r + 64, c : c + B].reshape(8, 8, B) * factor
+
+    sums_out(1)
+
+    @segment
+    def _():
+        logits(0, (5, 8), (0, 5))
+
+    text_sums_out(1)
+    shared("S", 5, 6, 7)
+
+    @segment
+    def _():
+        logits(0, (0, 8), (5, 8))
+
+    sums_out(0)
 
     @segment
     def _():
         for p in range(N):
             ist[:, p * B : (p + 1) * B] = is_[p * B : (p + 1) * B, :].T
 
-    half = 0.5 * LOGIT_SCALE
-    for slot in range(1, N):
-        sum_from(0, slot).wait_recv()
-    for mat in (0, 1):
-        for t in range(N):
-            r = mat * N + POS[t]
-            total = isum[r : r + 1, :]
-            for e in range(1, N):
-                q = mat * N + POS[minus(t, e)]
-                total = total + isum_in[e - 1, q : q + 1, :]
-            row_inv[mat, POS[t] * B : (POS[t] + 1) * B, :] = jnp.broadcast_to(half / total, (B, B)).T
-    for slot in range(1, N):
-        sum_from(1, slot).wait_recv()
-    for mat in (0, 1):
-        for t in range(N):
-            for par in (0, 1):
-                r = mat * 16 + 2 * POS[t] + par
-                total = csum[r : r + 1, :]
-                for e in range(1, N):
-                    q = mat * 16 + 2 * POS[minus(t, e)] + par
-                    total = total + tsum_in[e - 1, q : q + 1, :]
-                c = (2 * POS[t] + par) * B
-                col_inv[mat, :, c : c + B] = jnp.broadcast_to(half / total, (8, B))
+    text_sums_out(0)
+    sums_in(1)
+
+    @segment
+    def _():
+        for r in range(0, N * B, 64):
+            for c in range(0, 2 * N * B, B):
+                et[r : r + 64, c : c + B] = weighted(1, et, r, c).reshape(64, B)
+
+    sums_in(0)
 
     def weights(rows, cols):
         for r in range(rows[0] * B, rows[1] * B, 64):
             for c in range(cols[0] * 2 * B, cols[1] * 2 * B, B):
-                terms = []
-                for mat, e in ((0, es), (1, et)):
-                    factor = row_inv[mat, r : r + 64, :].reshape(8, 8, B) + col_inv[mat, :, c : c + B][None]
-                    terms.append(e[r : r + 64, c : c + B].reshape(8, 8, B) * factor)
-                w[r : r + 64, c : c + B] = (terms[0] - terms[1]).reshape(64, B).astype(BF16)
-
-    def grad_copy(side, slot):
+                term = weighted(0, es, r, c).reshape(64, B) - et[r : r + 64, c : c + B]
+                w[r : r + 64, c : c + B] = term.astype(BF16)
+
+    def halves(slot):
+        return (0, 1) if slot in HALVED else (None,)
+
+    def span(side, part):
+        rows = (B, 512)[side]
+        return (0, rows) if part is None else (part * rows // 2, rows // 2)
+
+    def grad_copy(side, slot, part):
+        first, rows = span(side, part)
         return remote(
-            (di_out, dt_out)[side].at[slot], (di_in, dt_in)[side].at[slot],
-            grad_send.at[side, slot], grad_recv.at[side, slot], peers[side](*GRAD_TO[slot]),
+            (di_out, dt_out)[side].at[slot, pl.ds(first, rows), :], (di_in, dt_in)[side].at[slot, pl.ds(first, rows), :],
+            grad_send.at[side, slot, part or 0], grad_recv.at[side, slot, part or 0], peers[side](*GRAD_TO[slot]),
         )
 
     def grad_sib(slot):
@@ -382,21 +441,29 @@
         for slot in slots:
             go(grad_sib(slot))
 
-    def total_of(side, slot):
+    def total_of(side, slot, part=None):
+        first, rows = span(side, part)
+        at = pl.ds(first, rows)
         if side == 0:
-            total = di_keep[slot]
+            total = di_keep[slot, at, :]
         else:
+            total = dt_keep[slot, at, :] + dt_sib[slot, at, :].astype(F32)
+        for source in SINKS.get(slot, ()):
+            for half_of in halves(source) if part is None else (part,):
+                grad_copy(side, source, half_of).wait_recv()
+            total = total + (di_in, dt_in)[side][source, at, :].astype(F32)
+        return total
+
+    def grad_sum_send(side, slot, part=None):
+        first, rows = span(side, part)
+        (di_out, dt_out)[side][slot, pl.ds(first, rows), :] = total_of(side, slot, part).astype(BF16)
+        go(grad_copy(side, slot, part))
+
+    def text_send(*slots):
+        for slot in slots:
             grad_sib(slot).wait_recv()
-            total = dt_keep[slot] + dt_sib[slot].astype(F32)
-        for source in SINKS.get(slot, ()):
-            grad_copy(side, source).wait_recv()
-            total = total + (di_in, dt_in)[side][source].astype(F32)
-        return total
-
-    def grad_send_from(side, *slots):
-        for slot in slots:
-            (di_out, dt_out)[side][slot] = total_of(side, slot).astype(BF16)
-            go(grad_copy(side, slot))
+            for part in halves(slot):
+                grad_sum_send(1, slot, part)
 
     def image_terms(p0, p1):
         out = jnp.dot(w[p0 * B : p1 * B, :], xs[...], preferred_element_type=F32)
@@ -409,64 +476,54 @@
 
     def image_send(*slots):
         for slot in slots:
-            go(grad_copy(0, slot))
-
-    @segment
-    def _():
-        weights((0, 8), (7, 8))
-        text_terms(7)
-
-    text_share(7)
-
-    @segment
-    def _():
-        weights((0, 8), (4, 6))
-        text_terms(5, 6)
-
-    text_share(5, 6)
-
-    @segment
-    def _():
-        weights((6, 8), (0, 4))
-        weights((6, 8), (6, 7))
-        image_terms(6, 8)
-
-    image_send(7)
-    grad_send_from(1, 7)
-
-    @segment
-    def _():
-        weights((4, 6), (0, 4))
-        weights((4, 6), (6, 7))
-        image_terms(4, 6)
-
-    image_send(5, 6)
-    grad_send_from(1, 5, 6)
-
-    @segment
-    def _():
-        weights((0, 4), (0, 4))
+            for part in halves(slot):
+                go(grad_copy(0, slot, part))
+
+    @segment
+    def _():
+        weights((0, 8), (5, 8))
+        text_terms(7, 5, 6)
+
+    text_share(7, 5, 6)
+
+    @segment
+    def _():
+        weights((5, 8), (0, 5))
+        image_terms(5, 8)
+
+    image_send(7, 5, 6)
+    text_send(7, 5, 6)
+
+    @segment
+    def _():
+        weights((0, 5), (0, 5))
         text_terms(2, 3)
 
     text_share(2, 3)
 
     @segment
     def _():
-        weights((0, 4), (6, 7))
-        image_terms(0, 4)
+        image_terms(1, 3)
 
     image_send(2, 3)
-    grad_send_from(1, 2, 3)
+    text_send(2, 3)
 
     @segment
     def _():
         text_terms(4, 1, 0)
 
     text_share(4, 1, 0)
-    grad_send_from(0, 4)
-    grad_send_from(1, 4)
-    grad_send_from(0, 1)
-    grad_send_from(1, 1)
+
+    @segment
+    def _():
+        image_terms(3, 5)
+        image_terms(0, 1)
+
+    grad_sum_send(0, 4)
+    text_send(4)
+    grad_sum_send(0, 1)
+    text_send(1)
+    grad_sib(0).wait_recv()
 
     def finish(raw, total):
         norm, inverse = unit_rows(raw)
@@ -484,7 +541,7 @@
     dma = pltpu.SemaphoreType.DMA
     return pl.pallas_call(
         kernel,
-        out_shape=(jax.ShapeDtypeStruct((B, 512), F32), jax.ShapeDtypeStruct((B, 512), F32)),
+        out_shape=(pltpu.VMEM((B, 512), F32), pltpu.VMEM((B, 512), F32)),
         in_specs=[anywhere] * 4,
         out_specs=(vmem, vmem),
         scratch_shapes=[
@@ -504,12 +561,12 @@
             pltpu.VMEM((2, 8, 2 * N * B), F32),
             pltpu.VMEM((2, N * B, B), F32),
             pltpu.VMEM((2, 8, 2 * N * B), F32),
-            pltpu.VMEM((16, B), F32),
-            pltpu.VMEM((7, 16, B), F32),
-            pltpu.VMEM((32, B), F32),
-            pltpu.VMEM((32, B), F32),
-            pltpu.VMEM((32, B), F32),
-            pltpu.VMEM((7, 32, B), F32),
+            pltpu.VMEM((2, N, B), F32),
+            pltpu.VMEM((2, 7, N, B), F32),
+            pltpu.VMEM((2, 2 * N, B), F32),
+            pltpu.VMEM((2, 2 * N, B), F32),
+            pltpu.VMEM((2, 2 * N, B), F32),
+            pltpu.VMEM((2, 7, 2 * N, B), F32),
             pltpu.VMEM((N, B, 512), F32),
             pltpu.VMEM((N, B, 512), BF16),
             pltpu.VMEM((N, B, 512), BF16),
@@ -523,10 +580,10 @@
             dma((2, N_HOPS)),
             dma((2, N)),
             dma((2, N)),
-            dma((15,)),
-            dma((15,)),
-            dma((2, N)),
-            dma((2, N)),
+            dma((2, 15)),
+            dma((2, 15)),
+            dma((2, N, 2)),
+            dma((2, N, 2)),
             dma((N,)),
             dma((N,)),
         ],

time: 59 us -> 56.9 us (0.964)
  local copies, waits for them, and re-layouts: 2.42 us -> 1.41 us
  Pallas kernels: 55.8 us -> 54.8 us
    pallas_call x1, Pallas kernels: 55.8 us -> 54.8 us  [per_device(): pl.pallas_call(kernel, out_shape=(pltpu.VMEM((B, 512), F32), pltpu.VMEM((...]
    unnamed x4 -> x2, local copies, waits for them, and re-layouts: 2.42 us -> 1.41 us
where the time goes in v4:
time: 56.9 us; the launch traced here: 56.8 us
  Pallas kernels  54.8 us (96%)
  local copies, waits for them, and re-layouts  1.41 us (2%)
  between operations  0.64 us (1%)
    pallas_call x1, Pallas kernels, per_device(): pl.pallas_call(kernel, out_shape=(pltpu.VMEM((B, 512), F32), pltpu.VMEM((...  54.8 us
    unnamed x2, local copies, waits for them, and re-layouts  1.41 us

profile of v4, /device:TPU:1, one launch (start us, length us, event | category | flops | bytes accessed | tf_op | source)
XLA Modules:
  0.0 56.8 jit_solution(10275233285616000475)
XLA Ops:
  0.6 54.8 %shard_map.59 = (f32[128,512]{1,0:T(8,128)S(1)}, f32[128,512]{1,0:T(8,128)S(1)}) custom-call(bf16[128,1024]{1,0:T(8,128)(2,1)} %ti_hbm.1, bf16[128,512]{1,0:T(8,128)(2,1)} %si_hbm.1, bf16[128,1024]{1,0:T(8,128)(2,1)} %tt_hbm.1, bf16[128,512]{1,0:T(8,128)(2,1)} %st_hbm.1), custom_call_target="tpu_custom_call" | custom-call | flops 10737418240 | bytes 1048576 | tf_op jit(solution)/shard_map/pallas_call | solution.py:542
  55.4 0.7 %copy.8 = f32[128,512]{1,0:T(8,128)} copy(f32[128,512]{1,0:T(8,128)S(1)} %get-tuple-element.2) | data formatting | bytes 524288
  56.1 0.7 %copy.9 = f32[128,512]{1,0:T(8,128)} copy(f32[128,512]{1,0:T(8,128)S(1)} %get-tuple-element.3) | data formatting | bytes 524288

commit v5 on v4

--- a/solution.py
+++ b/solution.py
@@ -183,24 +183,12 @@
     loads[1].wait()
     normalize(si_ref, is_, i0, 0, B)
     normalize(st_ref, xs, t0, 0, B)
-    pl.semaphore_wait(barrier, 7)
-    send((1, "S"))
     loads[2].wait()
     loads[3].wait()
-
-    @segment
-    def _():
-        normalize(ti_ref, it, i0, 0, 64)
-        normalize(tt_ref, xt, t0, 0, 64)
-
-    send((3, "T0"), (2, "T0"), (1, "T0"))
-
-    @segment
-    def _():
-        normalize(ti_ref, it, i0, 64, 64)
-        normalize(tt_ref, xt, t0, 64, 64)
-
-    send((3, "T1"), (2, "T1"), (3, "S"), (2, "S"))
+    normalize(ti_ref, it, i0, 0, B)
+    normalize(tt_ref, xt, t0, 0, B)
+    pl.semaphore_wait(barrier, 7)
+    send((1, "S"), (3, "T0"), (2, "T0"), (1, "T0"), (3, "T1"), (2, "T1"), (3, "S"), (2, "S"))
     share("T", 0)
     share("S", 0)
 
@@ -525,21 +513,24 @@
     text_send(1)
     grad_sib(0).wait_recv()
 
-    def finish(raw, total):
-        norm, inverse = unit_rows(raw)
-        return inverse * (total - norm * jnp.sum(norm * total, axis=1, keepdims=True))
-
-    gi_ref[...] = finish(si_ref[...], total_of(0, 0))
-    gt_ref[...] = finish(st_ref[...], total_of(1, 0).T)
+    gi_ref[...] = total_of(0, 0)
+    gt_ref[...] = total_of(1, 0).T
 
     for copy in started:
         copy.wait_send()
+
+
+def finish_kernel(si_ref, st_ref, di_ref, dt_ref, gi_ref, gt_ref):
+    for raw, total, out in ((si_ref, di_ref, gi_ref), (st_ref, dt_ref, gt_ref)):
+        norm, inverse = unit_rows(raw[...])
+        direction = total[...]
+        out[...] = inverse * (direction - norm * jnp.sum(norm * direction, axis=1, keepdims=True))
 
 
 def per_device(teacher_image, student_image, teacher_text, student_text):
     vmem, anywhere = pl.BlockSpec(memory_space=pltpu.VMEM), pl.BlockSpec(memory_space=pl.ANY)
     dma = pltpu.SemaphoreType.DMA
-    return pl.pallas_call(
+    directions = pl.pallas_call(
         kernel,
         out_shape=(pltpu.VMEM((B, 512), F32), pltpu.VMEM((B, 512), F32)),
         in_specs=[anywhere] * 4,
@@ -592,6 +583,14 @@
         ),
         cost_estimate=pl.CostEstimate(flops=10_737_418_240, bytes_accessed=1 << 20, transcendentals=1 << 22),
     )(teacher_image, student_image, teacher_text, student_text)
+    out = jax.ShapeDtypeStruct((B, 512), F32)
+    return pl.pallas_call(
+        finish_kernel,
+        out_shape=(out, out),
+        in_specs=[vmem] * 4,
+        out_specs=(vmem, vmem),
+        compiler_params=pltpu.CompilerParams(vmem_limit_bytes=4 << 20),
+    )(student_image, student_text, *directions)
 
 
 def solution(mesh):

time: 56.9 us -> 56.4 us (level)
  local copies, waits for them, and re-layouts: 1.41 us -> 0.01 us
  Pallas kernels: 54.8 us -> 55.6 us
    unnamed x2 -> x4, local copies, waits for them, and re-layouts: 1.41 us -> 0.01 us
    pallas_call x0 -> x1, Pallas kernels: none -> 0.99 us  [per_device(): pl.pallas_call(finish_kernel, out_shape=(out, out), in_specs=[vmem] * 4,...]
where the time goes in v5:
time: 56.4 us; the launch traced here: 56.3 us
  Pallas kernels  55.6 us (99%)
  between operations  0.67 us (1%)
    pallas_call x1, Pallas kernels, per_device(): pl.pallas_call(kernel, out_shape=(pltpu.VMEM((B, 512), F32), pltpu.VMEM((...  54.6 us

profile of v5, /device:TPU:1, one launch (start us, length us, event | category | flops | bytes accessed | tf_op | source)
XLA Modules:
  0.0 56.3 jit_solution(8566789282107073634)
XLA Ops:
  0.6 0.0 copy-start.1
  0.6 0.0 copy-start
  0.7 54.6 %shard_map.59 = (f32[128,512]{1,0:T(8,128)S(1)}, f32[128,512]{1,0:T(8,128)S(1)}) custom-call(bf16[128,1024]{1,0:T(8,128)(2,1)} %ti_hbm.1, bf16[128,512]{1,0:T(8,128)(2,1)} %si_ref.1, bf16[128,1024]{1,0:T(8,128)(2,1)} %tt_hbm.1, bf16[128,512]{1,0:T(8,128)(2,1)} %st_ref.1), custom_call_target="tpu_custom_call" | custom-call | flops 10737418240 | bytes 1048576 | tf_op jit(solution)/shard_map/pallas_call | solution.py:533
  55.3 0.0 copy-done.1
  55.3 0.0 copy-done
  55.3 1.0 %shard_map.60 = (f32[128,512]{1,0:T(8,128)}, f32[128,512]{1,0:T(8,128)}) custom-call(bf16[128,512]{1,0:T(8,128)(2,1)S(1)} %copy-done, bf16[128,512]{1,0:T(8,128)(2,1)S(1)} %copy-done.1, f32[128,512]{1,0:T(8,128)S(1)} %get-tuple-element.4.di_ref, f32[128,512]{1,0:T(8,128)S(1)} %get-tuple-element.5.dt_ref), custom_call_target="tpu_custom_call" | custom-call | tf_op jit(solution)/shard_map/pallas_call | solution.py:587
Async XLA Ops:
  0.6 54.6 %copy-start.1 = (bf16[128,512]{1,0:T(8,128)(2,1)S(1)}, bf16[128,512]{1,0:T(8,128)(2,1)}, u32[]{:S(2)}) copy-start(bf16[128,512]{1,0:T(8,128)(2,1)} %st_ref.1) | copy-start | bytes 393220
  0.6 54.6 %copy-start = (bf16[128,512]{1,0:T(8,128)(2,1)S(1)}, bf16[128,512]{1,0:T(8,128)(2,1)}, u32[]{:S(2)}) copy-start(bf16[128,512]{1,0:T(8,128)(2,1)} %si_ref.1) | copy-start | bytes 393220

commit v6 on v5

--- a/solution.py
+++ b/solution.py
@@ -101,6 +101,11 @@
         copy.start()
         started.append(copy)
 
+    def drain(count):
+        for copy in started[:count]:
+            copy.wait_send()
+        del started[:count]
+
     def remote(src, dst, send, recv, device):
         return pltpu.make_async_remote_copy(
             src_ref=src, dst_ref=dst, send_sem=send, recv_sem=recv, device_id=device, device_id_type=MESH
@@ -375,6 +380,7 @@
     def _():
         logits(0, (0, 8), (5, 8))
 
+    gathered = len(started)
     sums_out(0)
 
     @segment
@@ -383,6 +389,7 @@
             ist[:, p * B : (p + 1) * B] = is_[p * B : (p + 1) * B, :].T
 
     text_sums_out(0)
+    drain(gathered)
     sums_in(1)
 
     @segment
@@ -467,12 +474,21 @@
             for part in halves(slot):
                 go(grad_copy(0, slot, part))
 
-    @segment
-    def _():
-        weights((0, 8), (5, 8))
-        text_terms(7, 5, 6)
-
-    text_share(7, 5, 6)
+    summed = len(started)
+
+    @segment
+    def _():
+        weights((0, 8), (6, 8))
+        text_terms(5, 6)
+
+    text_share(5, 6)
+
+    @segment
+    def _():
+        weights((0, 8), (5, 6))
+        text_terms(7)
+
+    text_share(7)
 
     @segment
     def _():
@@ -480,44 +496,58 @@
         image_terms(5, 8)
 
     image_send(7, 5, 6)
-    text_send(7, 5, 6)
-
-    @segment
-    def _():
-        weights((0, 5), (0, 5))
+    text_send(5, 6, 7)
+
+    @segment
+    def _():
+        weights((0, 5), (1, 3))
         text_terms(2, 3)
 
     text_share(2, 3)
 
     @segment
     def _():
+        weights((0, 5), (0, 1))
+        weights((0, 5), (3, 5))
         image_terms(1, 3)
 
     image_send(2, 3)
+
+    @segment
+    def _():
+        text_terms(4, 1)
+
+    text_share(4, 1)
     text_send(2, 3)
 
     @segment
     def _():
-        text_terms(4, 1, 0)
-
-    text_share(4, 1, 0)
-
-    @segment
-    def _():
         image_terms(3, 5)
-        image_terms(0, 1)
-
+
+    drain(summed)
+    shared_terms = len(started)
     grad_sum_send(0, 4)
     text_send(4)
     grad_sum_send(0, 1)
     text_send(1)
+
+    @segment
+    def _():
+        text_terms(0)
+
+    text_share(0)
+
+    @segment
+    def _():
+        image_terms(0, 1)
+
     grad_sib(0).wait_recv()
+    drain(shared_terms)
 
     gi_ref[...] = total_of(0, 0)
     gt_ref[...] = total_of(1, 0).T
 
-    for copy in started:
-        copy.wait_send()
+    drain(len(started))
 
 
 def finish_kernel(si_ref, st_ref, di_ref, dt_ref, gi_ref, gt_ref):

time: 56.4 us -> 56.1 us (level)
  no operation moved by 1% of the time
where the time goes in v6:
time: 56.1 us; the launch traced here: 56 us
  Pallas kernels  55.3 us (99%)
  between operations  0.67 us (1%)
    pallas_call x1, Pallas kernels, per_device(): pl.pallas_call(kernel, out_shape=(pltpu.VMEM((B, 512), F32), pltpu.VMEM((...  54.3 us

profile of v6, /device:TPU:1, one launch (start us, length us, event | category | flops | bytes accessed | tf_op | source)
XLA Modules:
  0.0 56.0 jit_solution(16225212142155568125)
XLA Ops:
  0.6 0.0 copy-start.1
  0.6 0.0 copy-start
  0.7 54.3 %shard_map.59 = (f32[128,512]{1,0:T(8,128)S(1)}, f32[128,512]{1,0:T(8,128)S(1)}) custom-call(bf16[128,1024]{1,0:T(8,128)(2,1)} %ti_hbm.1, bf16[128,512]{1,0:T(8,128)(2,1)} %si_ref.1, bf16[128,1024]{1,0:T(8,128)(2,1)} %tt_hbm.1, bf16[128,512]{1,0:T(8,128)(2,1)} %st_ref.1), custom_call_target="tpu_custom_call" | custom-call | flops 10737418240 | bytes 1048576 | tf_op jit(solution)/shard_map/pallas_call | solution.py:563
  55.0 0.0 copy-done.1
  55.0 0.0 copy-done
  55.0 1.0 %shard_map.60 = (f32[128,512]{1,0:T(8,128)}, f32[128,512]{1,0:T(8,128)}) custom-call(bf16[128,512]{1,0:T(8,128)(2,1)S(1)} %copy-done, bf16[128,512]{1,0:T(8,128)(2,1)S(1)} %copy-done.1, f32[128,512]{1,0:T(8,128)S(1)} %get-tuple-element.4.di_ref, f32[128,512]{1,0:T(8,128)S(1)} %get-tuple-element.5.dt_ref), custom_call_target="tpu_custom_call" | custom-call | tf_op jit(solution)/shard_map/pallas_call | solution.py:617
Async XLA Ops:
  0.6 54.3 %copy-start.1 = (bf16[128,512]{1,0:T(8,128)(2,1)S(1)}, bf16[128,512]{1,0:T(8,128)(2,1)}, u32[]{:S(2)}) copy-start(bf16[128,512]{1,0:T(8,128)(2,1)} %st_ref.1) | copy-start | bytes 393220
  0.6 54.3 %copy-start = (bf16[128,512]{1,0:T(8,128)(2,1)S(1)}, bf16[128,512]{1,0:T(8,128)(2,1)}, u32[]{:S(2)}) copy-start(bf16[128,512]{1,0:T(8,128)(2,1)} %si_ref.1) | copy-start | bytes 393220

commit v7 on v6

--- a/solution.py
+++ b/solution.py
@@ -550,11 +550,15 @@
     drain(len(started))
 
 
-def finish_kernel(si_ref, st_ref, di_ref, dt_ref, gi_ref, gt_ref):
-    for raw, total, out in ((si_ref, di_ref, gi_ref), (st_ref, dt_ref, gt_ref)):
+def finish_kernel(si_ref, st_ref, di_ref, dt_ref, gi_hbm, gt_hbm, grads, sems):
+    copies = [pltpu.make_async_copy(grads.at[i], out, sems.at[i]) for i, out in enumerate((gi_hbm, gt_hbm))]
+    for i, (raw, total) in enumerate(((si_ref, di_ref), (st_ref, dt_ref))):
         norm, inverse = unit_rows(raw[...])
         direction = total[...]
-        out[...] = inverse * (direction - norm * jnp.sum(norm * direction, axis=1, keepdims=True))
+        grads[i] = inverse * (direction - norm * jnp.sum(norm * direction, axis=1, keepdims=True))
+        copies[i].start()
+    for copy in copies:
+        copy.wait()
 
 
 def per_device(teacher_image, student_image, teacher_text, student_text):
@@ -618,7 +622,8 @@
         finish_kernel,
         out_shape=(out, out),
         in_specs=[vmem] * 4,
-        out_specs=(vmem, vmem),
+        out_specs=(anywhere, anywhere),
+        scratch_shapes=[pltpu.VMEM((2, B, 512), F32), dma((2,))],
         compiler_params=pltpu.CompilerParams(vmem_limit_bytes=4 << 20),
     )(student_image, student_text, *directions)
 

time: 56.1 us -> 56.3 us (level)
  no operation moved by 1% of the time
where the time goes in v7:
time: 56.3 us; the launch traced here: 56.1 us
  Pallas kernels  55.3 us (98%)
  between operations  0.83 us (1%)
    pallas_call x1, Pallas kernels, per_device(): pl.pallas_call(kernel, out_shape=(pltpu.VMEM((B, 512), F32), pltpu.VMEM((...  54.3 us

profile of v7, /device:TPU:1, one launch (start us, length us, event | category | flops | bytes accessed | tf_op | source)
XLA Modules:
  0.0 56.1 jit_solution(17763919330782447814)
XLA Ops:
  0.6 0.0 copy-start.1
  0.6 0.0 copy-start
  0.7 54.3 %shard_map.59 = (f32[128,512]{1,0:T(8,128)S(1)}, f32[128,512]{1,0:T(8,128)S(1)}) custom-call(bf16[128,1024]{1,0:T(8,128)(2,1)} %ti_hbm.1, bf16[128,512]{1,0:T(8,128)(2,1)} %si_ref.1, bf16[128,1024]{1,0:T(8,128)(2,1)} %tt_hbm.1, bf16[128,512]{1,0:T(8,128)(2,1)} %st_ref.1), custom_call_target="tpu_custom_call" | custom-call | flops 10737418240 | bytes 1048576 | tf_op jit(solution)/shard_map/pallas_call | solution.py:567
  55.0 0.0 copy-done.1
  55.0 0.0 copy-done
  55.0 1.0 %shard_map.60 = (f32[128,512]{1,0:T(8,128)}, f32[128,512]{1,0:T(8,128)}) custom-call(bf16[128,512]{1,0:T(8,128)(2,1)S(1)} %copy-done, bf16[128,512]{1,0:T(8,128)(2,1)S(1)} %copy-done.1, f32[128,512]{1,0:T(8,128)S(1)} %get-tuple-element.4.di_ref, f32[128,512]{1,0:T(8,128)S(1)} %get-tuple-element.5.dt_ref), custom_call_target="tpu_custom_call" | custom-call | tf_op jit(solution)/shard_map/pallas_call | solution.py:621
Async XLA Ops:
  0.6 54.3 %copy-start.1 = (bf16[128,512]{1,0:T(8,128)(2,1)S(1)}, bf16[128,512]{1,0:T(8,128)(2,1)}, u32[]{:S(2)}) copy-start(bf16[128,512]{1,0:T(8,128)(2,1)} %st_ref.1) | copy-start | bytes 393220
  0.6 54.3 %copy-start = (bf16[128,512]{1,0:T(8,128)(2,1)S(1)}, bf16[128,512]{1,0:T(8,128)(2,1)}, u32[]{:S(2)}) copy-start(bf16[128,512]{1,0:T(8,128)(2,1)} %si_ref.1) | copy-start | bytes 393220
